TPU v7x, 32 devices: a whole 2x2x4 slice. The times are simulated.
32 devices in a mesh: dp: 8 (over z, y), seq: 4 (over x, core).
Axes of the slice: x: 2, y: 2, z: 4, core: 2. Of those that a mesh axis runs over, the one named last changes fastest.
Arguments:
- tokens: bfloat16 [128, 512, 768], P('dp', 'seq'), may hold values from -6 to 6
- sources: int32 [128], replicated, may hold values from 0 to 1, as said below
- lengths: int32 [128], P('dp'), may hold values from 64 to 512, as said below
- pairing: int32 [128], replicated, may hold values from 0 to 127, each once
- queries: bfloat16 [128, 768], P('dp'), may hold values from -6 to 6
- w_query: bfloat16 [768, 768], replicated, may hold values from -0.375 to 0.375
- b_query: float32 [768], replicated, may hold values from -1.5 to 1.5
- w_key: bfloat16 [768, 768], replicated, may hold values from -0.375 to 0.375
- w_value: bfloat16 [768, 768], replicated, may hold values from -0.21875 to 0.21875
- b_value: float32 [768], replicated, may hold values from -1.5 to 1.5
- w_out: bfloat16 [768, 768], replicated, may hold values from -0.4375 to 0.4375
- b_out: float32 [768], replicated, may hold values from -3 to 3
- gain_one: float32 [768], replicated, may hold values from 0.5 to 1.5
- shift_one: float32 [768], replicated, may hold values from -1 to 1
- w_up: bfloat16 [768, 3072], replicated, may hold values from -0.21875 to 0.21875
- b_up: float32 [3072], replicated, may hold values from -0.6 to 0.6
- w_down: bfloat16 [3072, 768], replicated, may hold values from -0.109375 to 0.109375
- second_feedforward_offset: float32 [768], replicated, may hold values from -3 to 3
- gain_two: float32 [768], replicated, may hold values from 0.5 to 1.5
- shift_two: float32 [768], replicated, may hold values from -1 to 1
Outputs:
- loss: float32 [], replicated
- activations: bfloat16 [128, 512, 768], P('dp', 'seq')
- grad_tokens: float32 [128, 512, 768], P('dp', 'seq')
- grad_w_query: float32 [768, 768], replicated
- grad_b_query: float32 [768], replicated
- grad_w_key: float32 [768, 768], replicated
- grad_w_value: float32 [768, 768], replicated
- grad_b_value: float32 [768], replicated
- grad_w_out: float32 [768, 768], replicated
- grad_b_out: float32 [768], replicated
- grad_gain_one: float32 [768], replicated
- grad_shift_one: float32 [768], replicated
- grad_w_up: float32 [768, 3072], replicated
- grad_b_up: float32 [3072], replicated
- grad_w_down: float32 [3072, 768], replicated
- grad_b_down: float32 [768], replicated
- grad_gain_two: float32 [768], replicated
- grad_shift_two: float32 [768], replicated
Inputs may be any that keep to these rules, and one draw needn't show every extreme that they name: Source 0 passages have lengths 512 // 8 to 256, source 1 passages 512 // 2 to 512; passage 0 has length 64 and passage 128 - 1 length 512. `sources`: passage 0 is of source 0 and passage 128 - 1 of source 1. `pairing`: each passage is the positive of exactly one query.
All inputs are finite; a program needn't handle non-finite values.
Results may differ from a plain program's by a relative error of at most 0.014.
The roundings to bfloat16 on the way count: a program that leaves them out, or rounds other values in their place, can miss the bound.
Values may be sent and summed in bfloat16 or wider, within the bound.
No kernel may reach another device: no remote copies, remote signals or barrier semaphores. Data moves between devices by JAX's collectives and lax.ppermute only.
A program may use at most 448 MiB of HBM per device.

v0:
```python
import jax
import jax.numpy as jnp
from jax import lax
from jax.sharding import PartitionSpec as P

HEADS = 12


largest_cosine_score = lax.Precision.HIGHEST
epsilon = 1e-05
contrast_sharpness_divisor = 0.01


def normalize(value):
    centred = value - jnp.mean(value, axis=-1, keepdims=True)
    inverse = lax.rsqrt(jnp.mean(centred * centred, axis=-1, keepdims=True) + epsilon)
    return (centred * inverse, inverse)


def norm_back(grad_unit, unit, inverse):
    first = jnp.mean(grad_unit, axis=-1, keepdims=True)
    second = jnp.mean(grad_unit * unit, axis=-1, keepdims=True)
    return inverse * (grad_unit - first - unit * second)


def project(left, weight):
    return jnp.einsum("ptd,de->pte", left, weight, preferred_element_type=jnp.float32)


def project_back(grad, weight):
    return jnp.einsum("pte,de->ptd", grad, weight, preferred_element_type=jnp.float32)


def outer_sum(left, grad):
    return jnp.einsum("ptd,pte->de", left, grad, preferred_element_type=jnp.float32)


def column_sum(grad):
    return jnp.sum(grad.astype(jnp.float32), axis=(0, 1))


def exact_gelu(value):
    return jax.nn.gelu(value, approximate=False)


def contrast(pooled_all, query_rows, targets, sources):
    document_unit_embedding = pooled_all * lax.rsqrt(
        jnp.sum(pooled_all * pooled_all, axis=-1, keepdims=True) + 1e-06
    )
    question_unit_embedding = query_rows * lax.rsqrt(
        jnp.sum(query_rows * query_rows, axis=-1, keepdims=True) + 1e-06
    )
    cosine_score_matrix = (
        jnp.dot(question_unit_embedding, document_unit_embedding.T, precision=largest_cosine_score)
        / contrast_sharpness_divisor
    )
    match = targets[:, None] == jnp.arange(pooled_all.shape[0], dtype=jnp.int32)[None, :]
    query_source = jnp.sum(jnp.where(match, sources[None, :], 0), axis=1)
    cosine_score_matrix = jnp.where(
        query_source[:, None] == sources[None, :], cosine_score_matrix, -1000000000.0
    )
    top = jnp.max(cosine_score_matrix, axis=1, keepdims=True)
    spread = top[:, 0] + jnp.log(jnp.sum(jnp.exp(cosine_score_matrix - top), axis=1))
    chosen = jnp.sum(jnp.where(match, cosine_score_matrix, 0.0), axis=1)
    return jnp.sum(spread - chosen)


def local(
    tokens,
    sources,
    lengths,
    pairing,
    queries,
    w_query,
    b_query,
    w_key,
    w_value,
    b_value,
    w_out,
    b_out,
    gain_one,
    shift_one,
    w_up,
    b_up,
    w_down,
    second_feedforward_offset,
    gain_two,
    shift_two,
):
    document_texts, block, width = tokens.shape
    head_size = width // HEADS
    span = block * lax.axis_size("seq")
    seq_at = lax.axis_index("seq")
    dp_at = lax.axis_index("dp")
    total_passages = document_texts * lax.axis_size("dp")
    scale = head_size ** (-0.5)
    place = seq_at * block + jnp.arange(block, dtype=jnp.int32)
    live_rows = (place[None, :] < lengths[:, None]).astype(jnp.float32)
    live_keys = jnp.arange(span, dtype=jnp.int32)[None, :] < lengths[:, None]
    inputs = tokens.astype(jnp.float32)
    query = (project(tokens, w_query) + b_query).astype(jnp.bfloat16)
    keyed = project(tokens, w_key).astype(jnp.bfloat16)
    valued = (project(tokens, w_value) + b_value).astype(jnp.bfloat16)
    key_all, value_all = (
        lax.all_gather(keyed, "seq", axis=1, tiled=True),
        lax.all_gather(valued, "seq", axis=1, tiled=True),
    )
    query_h = query.reshape(document_texts, block, HEADS, head_size)
    key_h = key_all.reshape(document_texts, span, HEADS, head_size)
    value_h = value_all.reshape(document_texts, span, HEADS, head_size)
    scores = (
        jnp.einsum("pqhd,pkhd->phqk", query_h, key_h, preferred_element_type=jnp.float32) * scale
    )
    scores = jnp.where(live_keys[:, None, None, :], scores, -1000000000.0)
    top = jnp.max(scores, axis=-1, keepdims=True)
    expo = jnp.exp(scores - top)
    expo_total = jnp.sum(expo, axis=-1, keepdims=True)
    probs = expo / expo_total
    probs_low = probs.astype(jnp.bfloat16)
    mixed = jnp.einsum("phqk,pkhd->pqhd", probs_low, value_h, preferred_element_type=jnp.float32)
    mixed = mixed.reshape(document_texts, block, width).astype(jnp.bfloat16)
    branch = project(mixed, w_out) + b_out
    unit_one, inverse_one = normalize(inputs + branch)
    hidden = unit_one * gain_one + shift_one
    hidden_low = hidden.astype(jnp.bfloat16)
    upward = project(hidden_low, w_up) + b_up
    gelu_value, gelu_back = jax.vjp(exact_gelu, upward)
    gelu_low = gelu_value.astype(jnp.bfloat16)
    downward = project(gelu_low, w_down) + second_feedforward_offset
    unit_two, inverse_two = normalize(hidden + downward)
    output = unit_two * gain_two + shift_two
    activations = output.astype(jnp.bfloat16)
    partial_pool = jnp.sum(live_rows[:, :, None] * output, axis=1)
    pool_total = lax.psum(partial_pool, "seq")
    counts = lengths.astype(jnp.float32)[:, None]
    pooled = pool_total / counts
    query_rows = queries.astype(jnp.float32)
    pooled_all, query_all = (
        lax.all_gather(pooled, "dp", axis=0, tiled=True),
        lax.all_gather(query_rows, "dp", axis=0, tiled=True),
    )
    whole_loss, loss_back = jax.vjp(
        lambda whole: contrast(whole, query_all, pairing, sources), pooled_all
    )
    (grad_all,) = loss_back(jnp.full_like(whole_loss, 1.0 / total_passages))
    loss = whole_loss / total_passages
    grad_pooled = lax.dynamic_slice_in_dim(grad_all, dp_at * document_texts, document_texts)
    grad_output = live_rows[:, :, None] * (grad_pooled / counts)[:, None, :]
    grad_gain_two = jnp.sum(grad_output * unit_two, axis=(0, 1))
    grad_shift_two = jnp.sum(grad_output, axis=(0, 1))
    grad_sum_two = norm_back(grad_output * gain_two, unit_two, inverse_two)
    grad_down_low = grad_sum_two.astype(jnp.bfloat16)
    grad_b_down = column_sum(grad_down_low)
    grad_w_down = outer_sum(gelu_low, grad_down_low)
    (grad_upward,) = gelu_back(project_back(grad_down_low, w_down))
    grad_up_low = grad_upward.astype(jnp.bfloat16)
    grad_b_up = column_sum(grad_up_low)
    grad_w_up = outer_sum(hidden_low, grad_up_low)
    grad_hidden = project_back(grad_up_low, w_up) + grad_sum_two
    grad_gain_one = jnp.sum(grad_hidden * unit_one, axis=(0, 1))
    grad_shift_one = jnp.sum(grad_hidden, axis=(0, 1))
    grad_sum_one = norm_back(grad_hidden * gain_one, unit_one, inverse_one)
    grad_branch_low = grad_sum_one.astype(jnp.bfloat16)
    grad_b_out = column_sum(grad_branch_low)
    grad_w_out = outer_sum(mixed, grad_branch_low)
    grad_mixed_flat = project_back(grad_branch_low, w_out).astype(jnp.bfloat16)
    grad_mixed = grad_mixed_flat.reshape(document_texts, block, HEADS, head_size)
    grad_probs = jnp.einsum(
        "pqhd,pkhd->phqk", grad_mixed, value_h, preferred_element_type=jnp.float32
    )
    row_delta = jnp.sum(probs * grad_probs, axis=-1, keepdims=True)
    grad_scores = probs * (grad_probs - row_delta)
    grad_scores_low = grad_scores.astype(jnp.bfloat16)
    grad_query = (
        jnp.einsum("phqk,pkhd->pqhd", grad_scores_low, key_h, preferred_element_type=jnp.float32)
        * scale
    )
    grad_query = grad_query.reshape(document_texts, block, width).astype(jnp.bfloat16)
    key_terms = jnp.einsum(
        "phqk,pqhd->pkhd", grad_scores_low, query_h, preferred_element_type=jnp.float32
    )
    key_terms = key_terms.reshape(document_texts, span, width) * scale
    value_terms = jnp.einsum(
        "phqk,pqhd->pkhd", probs_low, grad_mixed, preferred_element_type=jnp.float32
    )
    value_terms = value_terms.reshape(document_texts, span, width)
    key_summed, value_summed = (
        lax.psum_scatter(key_terms, "seq", scatter_dimension=1, tiled=True),
        lax.psum_scatter(value_terms, "seq", scatter_dimension=1, tiled=True),
    )
    grad_key = key_summed.astype(jnp.bfloat16)
    grad_value = value_summed.astype(jnp.bfloat16)
    grad_w_query = outer_sum(tokens, grad_query)
    grad_b_query = column_sum(grad_query)
    grad_w_key = outer_sum(tokens, grad_key)
    grad_w_value = outer_sum(tokens, grad_value)
    grad_b_value = column_sum(grad_value)
    grad_tokens = (
        project_back(grad_query, w_query)
        + project_back(grad_key, w_key)
        + project_back(grad_value, w_value)
        + grad_sum_one
    )
    hidden_units = grad_b_up.shape[0]
    small = jnp.concatenate(
        [
            grad_b_query,
            grad_b_value,
            grad_b_out,
            grad_gain_one,
            grad_shift_one,
            grad_b_up,
            grad_b_down,
            grad_gain_two,
            grad_shift_two,
        ]
    )
    flat_query = grad_w_query.reshape(-1)
    flat_key = grad_w_key.reshape(-1)
    flat_value = grad_w_value.reshape(-1)
    flat_out = grad_w_out.reshape(-1)
    flat_up = grad_w_up.reshape(-1)
    contracted_matrix_rows = grad_w_down.reshape(-1)
    part_a, part_b, part_c, part_d, part_e, part_f, part_g = (
        lax.psum_scatter(flat_query, ("dp", "seq"), scatter_dimension=0, tiled=True),
        lax.psum_scatter(flat_key, ("dp", "seq"), scatter_dimension=0, tiled=True),
        lax.psum_scatter(flat_value, ("dp", "seq"), scatter_dimension=0, tiled=True),
        lax.psum_scatter(flat_out, ("dp", "seq"), scatter_dimension=0, tiled=True),
        lax.psum_scatter(flat_up, ("dp", "seq"), scatter_dimension=0, tiled=True),
        lax.psum_scatter(contracted_matrix_rows, ("dp", "seq"), scatter_dimension=0, tiled=True),
        lax.psum_scatter(small, ("dp", "seq"), scatter_dimension=0, tiled=True),
    )
    sum_query, sum_key, sum_value, sum_out, upward_sum, sum_down, sum_small = (
        lax.all_gather(part_a.astype(jnp.bfloat16), ("dp", "seq"), axis=0, tiled=True).astype(
            part_a.dtype
        ),
        lax.all_gather(part_b.astype(jnp.bfloat16), ("dp", "seq"), axis=0, tiled=True).astype(
            part_b.dtype
        ),
        lax.all_gather(part_c.astype(jnp.bfloat16), ("dp", "seq"), axis=0, tiled=True).astype(
            part_c.dtype
        ),
        lax.all_gather(part_d.astype(jnp.bfloat16), ("dp", "seq"), axis=0, tiled=True).astype(
            part_d.dtype
        ),
        lax.all_gather(part_e.astype(jnp.bfloat16), ("dp", "seq"), axis=0, tiled=True).astype(
            part_e.dtype
        ),
        lax.all_gather(part_f.astype(jnp.bfloat16), ("dp", "seq"), axis=0, tiled=True).astype(
            part_f.dtype
        ),
        lax.all_gather(part_g.astype(jnp.bfloat16), ("dp", "seq"), axis=0, tiled=True).astype(
            part_g.dtype
        ),
    )
    offset = 0
    pieces = []
    for extent in (width, width, width, width, width, hidden_units, width, width, width):
        pieces.append(sum_small[offset : offset + extent])
        offset = offset + extent
    return (
        loss,
        activations,
        grad_tokens,
        sum_query.reshape(width, width),
        pieces[0],
        sum_key.reshape(width, width),
        sum_value.reshape(width, width),
        pieces[1],
        sum_out.reshape(width, width),
        pieces[2],
        pieces[3],
        pieces[4],
        upward_sum.reshape(width, hidden_units),
        pieces[5],
        sum_down.reshape(hidden_units, width),
        pieces[6],
        pieces[7],
        pieces[8],
    )


def solution(mesh):
    in_specs = (
        P("dp", "seq", None),
        P(),
        P("dp"),
        P(),
        P("dp", None),
        P(),
        P(),
        P(),
        P(),
        P(),
        P(),
        P(),
        P(),
        P(),
        P(),
        P(),
        P(),
        P(),
        P(),
        P(),
    )
    out_specs = (
        P(),
        P("dp", "seq", None),
        P("dp", "seq", None),
        P(),
        P(),
        P(),
        P(),
        P(),
        P(),
        P(),
        P(),
        P(),
        P(),
        P(),
        P(),
        P(),
        P(),
        P(),
    )
    return jax.shard_map(local, mesh=mesh, in_specs=in_specs, out_specs=out_specs, check_vma=False)
```

profile of v0, /device:TPU:0, one launch (start us, length us, event | category | flops | bytes accessed | tf_op | source)
XLA Modules:
  0.0 1696.1 jit_solution(17513423611221872729)
XLA Ops:
  33.3 33.3 %all_gather.33 = f32[128,768]{1,0:T(8,128)S(1)} all-gather(f32[16,768]{1,0:T(8,128)S(1)} %convert_element_type.128), channel_id=1, replica_groups=mesh['dp'=8,'seq'=4] {'dp'}, dimensions={0}, use_global_device_ids=true | all-gather | bytes 442368 | tf_op jit(solution)/shard_map/all_gather | solution.py:140
  68.7 30.2 %all-gather.11.cloned.1.call-done = bf16[16,512,768]{2,1,0:T(8,128)(2,1)} async-done(((bf16[16,128,768]{2,1,0:T(8,128)(2,1)}), bf16[16,512,768]{2,1,0:T(8,128)(2,1)}) %all-gather.11.cloned.1.call-update) | async-done | bytes 12582928 | tf_op jit(solution)/shard_map/all_gather | solution.py:105
  98.9 17.2 %copy.67 = bf16[16,512,768]{1,2,0:T(8,128)(2,1)} copy(bf16[16,512,768]{2,1,0:T(8,128)(2,1)} %all-gather.11.cloned.1.call-done) | data formatting | bytes 25165824 | tf_op jit(solution)/shard_map/all_gather | solution.py:105
  116.1 26.1 %fusion.96 = (f32[16,12,128]{2,1,0:T(8,128)S(1)}, f32[16,12,128,512]{3,2,1,0:T(8,128)}) fusion(pred[16,512]{1,0:T(8,128)(4,1)S(1)} %iota_compare_fusion.2, bf16[16,128,12,64]{1,3,2,0:T(8,128)(2,1)} %bitcast.117, bf16[16,512,12,64]{1,3,2,0:T(8,128)(2,1)} %bitcast.113), kind=kOutput, calls=%fused_computation.186 | convolution fusion | flops 1660944896 | bytes 66166784 | tf_op jit(solution)/shard_map/sub | solution.py:116
  142.2 41.0 %all-gather.9.cloned.1.call-done = bf16[16,512,768]{2,1,0:T(8,128)(2,1)} async-done(((bf16[16,128,768]{2,1,0:T(8,128)(2,1)}), bf16[16,512,768]{2,1,0:T(8,128)(2,1)}) %all-gather.9.cloned.1.call-update) | async-done | bytes 12582928 | tf_op jit(solution)/shard_map/all_gather | solution.py:106
  199.9 23.5 %fusion.37 = bf16[16,12,64,128]{3,2,1,0:T(8,128)(2,1)} fusion(bf16[16,512,12,64]{1,3,2,0:T(8,128)(2,1)} %bitcast.119, f32[16,12,128,512]{3,2,1,0:T(8,128)} %get-tuple-element.55, f32[16,12,128]{2,1,0:T(8,128)S(1)} %get-tuple-element.54), kind=kOutput, calls=%fused_computation.84 | convolution fusion | flops 1637351424 | bytes 66158592 | tf_op jit(solution)/shard_map/phqk,pkhd->pqhd/dot_general | solution.py:120
  229.5 23.3 %fusion.16 = (u16[128,3072]{1,0:T(8,128)(2,1)S(1)}, u16[128,3072]{1,0:T(8,128)(2,1)S(1)}, f32[16,128,3072]{2,1,0:T(8,128)}) fusion(f32[3072]{0:T(1024)S(1)} %copy-done.33, bf16[768,3072]{1,0:T(8,128)(2,1)} %param.34, f32[16,128,768]{2,1,0:T(8,128)S(1)} %get-tuple-element.57, f32[768]{0:T(1024)S(1)} %copy-done.53, f32[768]{0:T(1024)S(1)} %copy-done.24, ...), kind=kOutput, calls=%fused_computation.38 | convolution fusion | flops 9758834688 | bytes 37783552 | tf_op jit(solution)/shard_map/ptd,de->pte/dot_general | solution.py:27
  252.8 60.3 %multiply_convert_fusion.1 = (bf16[16,128,3072]{2,1,0:T(8,128)(2,1)}, f32[16,128,3072]{2,1,0:T(8,128)}) fusion(f32[16,128,3072]{2,1,0:T(8,128)} %get-tuple-element.58, f32[3072]{0:T(1024)S(1)} %copy-done.33, u16[128,3072]{1,0:T(8,128)(2,1)S(1)} %get-tuple-element.19, u16[128,3072]{1,0:T(8,128)(2,1)S(1)} %get-tuple-element.18), kind=kLoop, calls=%fused_computation.15 | loop fusion | flops 446693376 | bytes 64499712 | tf_op jit(solution)/shard_map/convert_element_type | solution.py:128
  343.0 31.5 %all_gather.36 = f32[128,768]{1,0:T(8,128)S(1)} all-gather(f32[16,768]{1,0:T(8,128)S(1)} %broadcast_divide_fusion.1), channel_id=1, replica_groups=mesh['dp'=8,'seq'=4] {'dp'}, dimensions={0}, use_global_device_ids=true | all-gather | bytes 442368 | tf_op jit(solution)/shard_map/all_gather | solution.py:139
  386.6 33.5 %convert_reduce_fusion = (f32[3072]{0:T(1024)}, bf16[16,128,3072]{2,1,0:T(8,128)(2,1)}) fusion(f32[16,128,3072]{2,1,0:T(8,128)} %get-tuple-element.43, bf16[16,128,768]{2,1,0:T(8,128)(2,1)} %get-tuple-element.39, bf16[3072,768]{1,0:T(8,128)(2,1)} %param.36, f32[16,128,3072]{2,1,0:T(8,128)} %get-tuple-element.58, f32[3072]{0:T(1024)S(1)} %copy-done.33), kind=kOutput, calls=%fused_computation.13 | convolution fusion | flops 9770628096 | bytes 70803456 | tf_op jit(solution)/shard_map/pte,de->ptd/dot_general | solution.py:31
  420.0 21.5 %multiply_reduce_fusion.2 = (f32[768]{0:T(1024)}, f32[16,128]{1,0:T(8,128)S(1)}, f32[16,128]{1,0:T(8,128)S(1)}, f32[768]{0:T(1024)}, f32[16,128,768]{2,1,0:T(8,128)}) fusion(f32[16,128,768]{2,1,0:T(8,128)} %copy-done.4, f32[16,128]{1,0:T(8,128)S(1)} %add_rsqrt_fusion.1, f32[16,128]{1,0:T(8,128)S(1)} %broadcast_multiply_fusion.6, f32[768]{0:T(1024)S(1)} %copy-done.24, ...), kind=kOutput, calls=%fused_computation.50 | convolution fusion | flops 9691981824 | bytes 36311040 | tf_op jit(solution)/shard_map/pte,de->ptd/dot_general | solution.py:31
  458.2 26.8 %fusion.11 = f32[16,12,64,512]{3,2,1,0:T(8,128)} fusion(bf16[16,128,12,64]{1,3,2,0:T(8,128)(2,1)} %bitcast.123, f32[16,12,128,512]{3,2,1,0:T(8,128)} %get-tuple-element.55, f32[16,12,128]{2,1,0:T(8,128)S(1)} %copy-done.15), kind=kOutput, calls=%fused_computation.33 | convolution fusion | flops 1635778560 | bytes 78741504 | tf_op jit(solution)/shard_map/phqk,pqhd->pkhd/dot_general | solution.py:183
  485.1 47.3 %multiply_reduce_fusion = (f32[16,12,128]{2,1,0:T(8,128)S(1)}, f32[16,12,128,512]{3,2,1,0:T(8,128)}) fusion(f32[16,12,128,512]{3,2,1,0:T(8,128)} %get-tuple-element.55, f32[16,12,128]{2,1,0:T(8,128)S(1)} %copy-done.15, bf16[16,128,12,64]{1,3,2,0:T(8,128)(2,1)} %bitcast.124, bf16[16,512,12,64]{1,3,2,0:T(8,128)(2,1)} %bitcast.120), kind=kOutput, calls=%fused_computation.2 | convolution fusion | flops 1648336896 | bytes 116588544 | tf_op jit(solution)/shard_map/pqhd,pkhd->phqk/dot_general | solution.py:168
  532.4 41.4 %multiply_convert_fusion = bf16[16,12,128,512]{3,2,1,0:T(8,128)(2,1)} fusion(f32[16,12,128,512]{3,2,1,0:T(8,128)} %get-tuple-element.67, f32[16,12,128]{2,1,0:T(8,128)S(1)} %get-tuple-element.66, f32[16,12,128,512]{3,2,1,0:T(8,128)} %get-tuple-element.55, f32[16,12,128]{2,1,0:T(8,128)S(1)} %copy-done.15), kind=kLoop, calls=%fused_computation.1 | loop fusion | flops 50331648 | bytes 126025728 | tf_op jit(solution)/shard_map/convert_element_type | solution.py:173
  573.8 17.7 %broadcast_multiply_fusion = f32[16,12,64,512]{3,2,1,0:T(8,128)} fusion(bf16[16,128,12,64]{1,3,2,0:T(8,128)(2,1)} %bitcast.118, bf16[16,12,128,512]{3,2,1,0:T(8,128)(2,1)} %multiply_convert_fusion), kind=kOutput, calls=%fused_computation.32 | convolution fusion | flops 1616904192 | bytes 53477376 | tf_op jit(solution)/shard_map/phqk,pqhd->pkhd/dot_general | solution.py:179
  650.8 17.2 %convert_reduce_fusion.4 = (f32[12,64]{1,0:T(8,128)S(1)}, bf16[16,12,64,128]{3,2,1,0:T(8,128)(2,1)}) fusion(bf16[16,512,12,64]{1,3,2,0:T(8,128)(2,1)} %bitcast.114, bf16[16,12,128,512]{3,2,1,0:T(8,128)(2,1)} %multiply_convert_fusion), kind=kOutput, calls=%fused_computation.53 | convolution fusion | flops 1616903424 | bytes 40897536 | tf_op jit(solution)/shard_map/phqk,pkhd->pqhd/dot_general | solution.py:175
  702.5 147.2 %reduce-scatter.3.cloned.1.call-done = f32[16,128,768]{1,2,0:T(8,128)} async-done(((f32[16,512,768]{1,2,0:T(8,128)}), f32[16,128,768]{1,2,0:T(8,128)}) %reduce-scatter.3.cloned.1.call-update) | async-done | bytes 6291472 | tf_op jit(solution)/shard_map/reduce_scatter | solution.py:188
  862.6 461.8 %all-reduce.10 = (bf16[589824]{0:T(1024)(128)(2,1)}, bf16[9216]{0:T(1024)(128)(2,1)S(1)}, bf16[589824]{0:T(1024)(128)(2,1)}, bf16[589824]{0:T(1024)(128)(2,1)}, ...) all-reduce(f32[589824]{0:T(1024)} %reshape.248, ...), channel_id=4, replica_groups=mesh['dp'=8,'seq'=4] {'dp','seq'}, use_global_device_ids=true, to_apply=%region_25.26.clone | all-reduce | flops 7087104 | bytes 42522624
  1342.9 38.1 %all-reduce = bf16[9216]{0:T(1024)(128)(2,1)S(1)} all-reduce(bf16[9216]{0:T(1024)(128)(2,1)S(1)} %dynamic-update-slice), channel_id=1, replica_groups=mesh['dp'=8,'seq'=4] {'dp','seq'}, use_global_device_ids=true, to_apply=%add | all-reduce | flops 9216 | bytes 36864
  1406.8 27.8 %all-gather.19.cloned.1.call-done = bf16[589824]{0:T(1024)(128)(2,1)} async-done(((bf16[18432]{0:T(1024)(128)(2,1)}), bf16[589824]{0:T(1024)(128)(2,1)}) %all-gather.19.cloned.1.call-update) | async-done | bytes 1179664 | tf_op jit(solution)/shard_map/all_gather | solution.py:243
  1438.0 52.5 %all-gather.15.cloned.1.call-done = bf16[589824]{0:T(1024)(128)(2,1)} async-done(((bf16[18432]{0:T(1024)(128)(2,1)}), bf16[589824]{0:T(1024)(128)(2,1)}) %all-gather.15.cloned.1.call-update) | async-done | bytes 1179664 | tf_op jit(solution)/shard_map/all_gather | solution.py:237
  1493.9 53.1 %all-gather.13.cloned.1.call-done = bf16[589824]{0:T(1024)(128)(2,1)} async-done(((bf16[18432]{0:T(1024)(128)(2,1)}), bf16[589824]{0:T(1024)(128)(2,1)}) %all-gather.13.cloned.1.call-update) | async-done | bytes 1179664 | tf_op jit(solution)/shard_map/all_gather | solution.py:234
  1550.3 62.1 %all-gather.21.cloned.1.call-done = bf16[2359296]{0:T(1024)(128)(2,1)} async-done(((bf16[73728]{0:T(1024)(128)(2,1)}), bf16[2359296]{0:T(1024)(128)(2,1)}) %all-gather.21.cloned.1.call-update) | async-done | bytes 4718608 | tf_op jit(solution)/shard_map/all_gather | solution.py:246
  1621.3 56.4 %all-gather.23.cloned.1.call-done = bf16[2359296]{0:T(1024)(128)(2,1)} async-done(((bf16[73728]{0:T(1024)(128)(2,1)}), bf16[2359296]{0:T(1024)(128)(2,1)}) %all-gather.23.cloned.1.call-update) | async-done | bytes 4718608 | tf_op jit(solution)/shard_map/all_gather | solution.py:249
  (229 shorter events, 288.0 us)
Async XLA Ops:
  7.2 216.2 %copy-start = (bf16[768,768]{1,0:T(8,128)(2,1)S(1)}, bf16[768,768]{1,0:T(8,128)(2,1)}, u32[]{:S(2)}) copy-start(bf16[768,768]{1,0:T(8,128)(2,1)} %param.30) | copy-start | bytes 3538948
  7.2 91.7 %all-gather.11.cloned.1.call-start = ((), (), s32[]{:S(2)}) async-start(), calls=%async_computation.3 | async-start | bytes 15728640 | tf_op jit(solution)/shard_map/all_gather | solution.py:105
  14.0 169.2 %all-gather.9.cloned.1.call-start = ((), (), s32[]{:S(2)}) async-start(), calls=%async_computation.2 | async-start | bytes 15728640 | tf_op jit(solution)/shard_map/all_gather | solution.py:106
  20.3 661.7 %reduce-scatter.5.cloned.1.call-start = ((), (), s32[]{:S(2)}) async-start(), calls=%async_computation.5 | async-start | bytes 31457280 | tf_op jit(solution)/shard_map/reduce_scatter | solution.py:189
  142.2 57.7 %copy-start.14 = (f32[16,12,128]{2,1,0:T(8,128)}, f32[16,12,128]{2,1,0:T(8,128)S(1)}, u32[]{:S(2)}) copy-start(f32[16,12,128]{2,1,0:T(8,128)S(1)} %get-tuple-element.54) | copy-start | bytes 294916
  228.5 84.6 %copy-start.4 = (f32[16,128,768]{2,1,0:T(8,128)}, f32[16,128,768]{2,1,0:T(8,128)S(1)}, u32[]{:S(2)}) copy-start(f32[16,128,768]{2,1,0:T(8,128)S(1)} %get-tuple-element.57) | copy-start | bytes 18874372
  228.6 212.9 %copy-start.11 = (f32[16,128]{1,0:T(8,128)}, f32[16,128]{1,0:T(8,128)S(1)}, u32[]{:S(2)}) copy-start(f32[16,128]{1,0:T(8,128)S(1)} %broadcast_multiply_fusion.6) | copy-start | bytes 24580
  229.5 212.1 %copy-start.16 = (f32[16,128]{1,0:T(8,128)}, f32[16,128]{1,0:T(8,128)S(1)}, u32[]{:S(2)}) copy-start(f32[16,128]{1,0:T(8,128)S(1)} %add_rsqrt_fusion.1) | copy-start | bytes 24580
  252.8 60.3 %copy-start.52 = (f32[768]{0:T(1024)S(1)}, f32[768]{0:T(1024)}, u32[]{:S(2)}) copy-start(f32[768]{0:T(1024)} %param.37) | copy-start | bytes 9220
  329.0 45.7 %copy-start.6 = (f32[128,768]{1,0:T(8,128)S(1)}, f32[128,768]{1,0:T(8,128)}, u32[]{:S(2)}) copy-start(f32[128,768]{1,0:T(8,128)} %copy-done.5) | copy-start | bytes 1179652
  329.1 45.6 %copy-start.40 = (s32[128]{0:T(128)S(1)}, s32[128]{0:T(128)}, u32[]{:S(2)}) copy-start(s32[128]{0:T(128)} %param.21) | copy-start | bytes 1540
  329.1 46.3 %copy-start.42 = (s32[128]{0:T(128)S(1)}, s32[128]{0:T(128)}, u32[]{:S(2)}) copy-start(s32[128]{0:T(128)} %param.23) | copy-start | bytes 1540
  485.1 364.6 %reduce-scatter.3.cloned.1.call-start = ((), (), s32[]{:S(2)}) async-start(), calls=%async_computation.4 | async-start | bytes 31457280 | tf_op jit(solution)/shard_map/reduce_scatter | solution.py:188
  591.5 812.0 %all-gather.17.cloned.1.call-start = ((), (), s32[]{:S(2)}) async-start(), calls=%async_computation.8 | async-start | bytes 1216512 | tf_op jit(solution)/shard_map/all_gather | solution.py:240
  862.6 471.0 %copy-start.32 = (f32[128]{0:T(128)S(1)}, f32[128]{0:T(128)}, u32[]{:S(2)}) copy-start(f32[128]{0:T(128)} %copy-done.31) | copy-start | bytes 1540
  862.6 471.0 %copy-start.47 = (f32[128]{0:T(128)S(1)}, f32[128]{0:T(128)}, u32[]{:S(2)}) copy-start(f32[128]{0:T(128)} %copy-done.46) | copy-start | bytes 1540
  862.6 471.0 %copy-start.48 = (f32[128]{0:T(128)S(1)}, f32[128]{0:T(128)}, u32[]{:S(2)}) copy-start(f32[128]{0:T(128)} %get-tuple-element.28) | copy-start | bytes 1540
  1325.8 108.8 %all-gather.19.cloned.1.call-start = ((), (), s32[]{:S(2)}) async-start(), calls=%async_computation.9 | async-start | bytes 1216512 | tf_op jit(solution)/shard_map/all_gather | solution.py:243
  1327.3 163.2 %all-gather.15.cloned.1.call-start = ((), (), s32[]{:S(2)}) async-start(), calls=%async_computation.7 | async-start | bytes 1216512 | tf_op jit(solution)/shard_map/all_gather | solution.py:237
  1328.8 218.2 %all-gather.13.cloned.1.call-start = ((), (), s32[]{:S(2)}) async-start(), calls=%async_computation.6 | async-start | bytes 1216512 | tf_op jit(solution)/shard_map/all_gather | solution.py:234
  1330.2 282.2 %all-gather.21.cloned.1.call-start = ((), (), s32[]{:S(2)}) async-start(), calls=%async_computation.10 | async-start | bytes 4866048 | tf_op jit(solution)/shard_map/all_gather | solution.py:246
  1331.9 345.8 %all-gather.23.cloned.1.call-start = ((), (), s32[]{:S(2)}) async-start(), calls=%async_computation.11 | async-start | bytes 4866048 | tf_op jit(solution)/shard_map/all_gather | solution.py:249
  1334.8 56.0 %slice-start = ((s8[6291456]{0:T(1024)(128)(4,1)}), s8[2097152]{0:T(1024)(128)(4,1)S(1)}, s32[]{:S(2)}) async-start(s8[6291456]{0:T(1024)(128)(4,1)} %bitcast.111), calls=%async_computation.12 | async-start | bytes 4194304
  1612.5 75.2 %copy-start.1 = (bf16[768,768]{1,0:T(8,128)(2,1)S(1)}, bf16[768,768]{1,0:T(8,128)(2,1)}, u32[]{:S(2)}) copy-start(bf16[768,768]{1,0:T(8,128)(2,1)} %param.30) | copy-start | bytes 3538948
  (43 other events, 419.5 us)
Sparse Core Ops, SparseCore 0:
  14.1 84.7 all-gather.10
  101.0 82.0 all-gather.8
  485.2 181.3 reduce-scatter.4
  669.2 180.3 reduce-scatter.2
  1326.0 52.8 all-gather.16
  1381.6 52.9 all-gather.18
  1437.5 52.9 all-gather.14
  1494.0 52.9 all-gather.12
  1549.9 62.5 all-gather.20
  1615.2 62.4 all-gather.22
where the time goes:
time: 1700 us
  blocking collectives  575 us (34%)
  waiting for transfers between devices  471 us (28%)
  matrix products  373 us (22%)
  other arithmetic  131 us (8%)
  local copies, waits for them, and re-layouts  128 us (8%)
  between operations  17.3 us (1%)
    unnamed x2, blocking collectives  500 us
    reduce_scatter x1, waiting for transfers between devices, local(): lax.psum_scatter(key_terms, 'seq', scatter_dimension=1, tiled=True)  147 us
    dot_general x6, matrix products, project_back(): jnp.einsum('pte,de->ptd', grad, weight, preferred_element_type=jnp.float32)  87.8 us
    dot_general x6, matrix products, project(): jnp.einsum('ptd,de->pte', left, weight, preferred_element_type=jnp.float32)  63.1 us
    dot_general x6, matrix products, outer_sum(): jnp.einsum('ptd,pte->de', left, grad, preferred_element_type=jnp.float32)  62.2 us
    all_gather x1, waiting for transfers between devices, local(): lax.all_gather(part_e.astype(jnp.bfloat16), ('dp', 'seq'), axis=0, tiled=...  62.1 us
    convert_element_type x1, other arithmetic, local(): gelu_low = gelu_value.astype(jnp.bfloat16)  60.3 us
    all_gather x1, waiting for transfers between devices, local(): lax.all_gather(part_f.astype(jnp.bfloat16), ('dp', 'seq'), axis=0, tiled=...  56.4 us
  transfers between devices with their start and end apart: 10, of which 8 were waited for; matrix products, arithmetic and copies ran while one was open for 20% of the time, Pallas kernels for 0%

commit v1 on v0

v1 whole, which is shorter than its diff:
```python
import jax
import jax.numpy as jnp
from jax import lax
from jax.experimental import pallas as pl
from jax.experimental.pallas import tpu as pltpu
from jax.sharding import PartitionSpec as P

HEADS = 12
EPS = 1e-05
TEMPERATURE = 0.01
MASKED = -1000000000.0
BOTH = ("dp", "seq")
EXACT = lax.Precision.HIGHEST
BF = jnp.bfloat16
F32 = jnp.float32
VMEM_BYTES = 60 * 2**20
BRIEF = pl.CostEstimate(flops=7 * 10**10, bytes_accessed=10**6, transcendentals=0)
TICK = pl.CostEstimate(flops=1000, bytes_accessed=1000, transcendentals=0)


def dot(left, right, left_at=1, right_at=0):
    return lax.dot_general(
        left, right, (((left_at,), (right_at,)), ((), ())), preferred_element_type=F32
    )


def normalize(value):
    centred = value - jnp.mean(value, axis=-1, keepdims=True)
    inverse = lax.rsqrt(jnp.mean(centred * centred, axis=-1, keepdims=True) + EPS)
    return centred * inverse, inverse


def norm_back(grad_unit, unit, inverse):
    first = jnp.mean(grad_unit, axis=-1, keepdims=True)
    second = jnp.mean(grad_unit * unit, axis=-1, keepdims=True)
    return inverse * (grad_unit - first - unit * second)


def gelu_and_slope(value):
    size = jnp.abs(value)
    t = 1.0 / (1.0 + (0.3275911 * 0.7071067811865476) * size)
    bell = jnp.exp(-0.5 * (value * value))
    tail = (
        (((0.5 * 1.061405429 * t - 0.5 * 1.453152027) * t + 0.5 * 1.421413741) * t
         - 0.5 * 0.284496736) * t + 0.5 * 0.254829592
    ) * t * bell
    below = jnp.where(value >= 0.0, 1.0 - tail, tail)
    return value * below, below + value * (bell * 0.3989422804014327)


def lane_half(width, which):
    lanes = lax.broadcasted_iota(jnp.int32, (1, width), 1)
    return ((lanes >= which * (width // 2)) & (lanes < (which + 1) * (width // 2))).astype(F32)


def whole(shape):
    return pl.BlockSpec(shape, lambda i, *_: (0,) * len(shape))


def per_passage(shape, first=0):
    return pl.BlockSpec((1,) + tuple(shape), lambda i, *_: (i + first,) + (0,) * len(shape))


ANYWHERE = pl.BlockSpec(memory_space=pl.ANY)


def fetch(sources, targets, sems):
    return [
        pltpu.make_async_copy(s, t, sems.at[i]) for i, (s, t) in enumerate(zip(sources, targets))
    ]


def forward_kernel(lens, src, *refs, pieces, first, aliased, riders):
    refs = list(refs)
    take = lambda n: [refs.pop(0) for _ in range(n)]
    x_in = take(pieces)
    hbm = take(6)
    (vectors,) = take(1)
    take(aliased + riders)
    (x_all, q_out, k_out, v_out, mixed_out, lse_out, unit_one_out, inverse_one_out,
     hidden_low_out, gelu_out, slope_out, unit_two_out, inverse_two_out, sums_out) = take(14)
    act = take(pieces)
    take(riders)
    held = take(6)
    act_held, sems = take(2)
    w_query, w_key, w_value, w_out, w_up, w_down = held
    b_query, b_value, b_out, gain_one, shift_one, b_down, gain_two, shift_two = (
        vectors[n : n + 1, :] for n in range(8)
    )
    step = pl.program_id(0)
    copies = fetch(hbm, held, sems)

    @pl.when(step == 0)
    def _():
        for copy in copies:
            copy.start()

    def ready(*which):
        @pl.when(step == 0)
        def _():
            for i in which:
                copies[i].wait()

    span, width = x_all.shape[1:]
    block = span // pieces
    head = width // HEADS
    pair = 2 * head
    length = lens[first + step]
    for k in range(pieces):
        x_all[0, pl.ds(pl.multiple_of(src[k] * block, block), block), :] = x_in[k][0]
    x = x_all[0]
    ready(0, 1, 2)
    q_out[0] = ((dot(x, w_query[...]) + b_query) * (head ** -0.5)).astype(BF)
    k_out[0] = dot(x, w_key[...]).astype(BF)
    v_out[0] = (dot(x, w_value[...]) + b_value).astype(BF)
    key_mask = jnp.where(
        lax.broadcasted_iota(jnp.int32, (1, span), 1) < length, 0.0, MASKED
    ).astype(F32)
    lanes = lax.broadcasted_iota(jnp.int32, (1, 128), 1)
    stats = jnp.zeros((span, 128), F32)
    for p in range(HEADS // 2):
        at = slice(p * pair, (p + 1) * pair)
        qp, kp, vp = q_out[0, :, at], k_out[0, :, at], v_out[0, :, at]
        total = None
        for h in range(2):
            half = lane_half(pair, h).astype(BF)
            scores = dot(qp, kp * half, 1, 1) + key_mask
            top = jnp.max(scores, axis=-1, keepdims=True)
            expo = jnp.exp(scores - top)
            norm = jnp.sum(expo, axis=-1, keepdims=True)
            low = (expo * (1.0 / norm)).astype(BF)
            term = dot(low, vp * half)
            total = term if total is None else total + term
            stats = jnp.where(lanes == 2 * p + h, top + jnp.log(norm), stats)
        mixed_out[0, :, at] = total.astype(BF)
    lse_out[0] = stats.T[: lse_out.shape[1]]
    ready(3)
    unit_one, inverse_one = normalize(x.astype(F32) + (dot(mixed_out[0], w_out[...]) + b_out))
    unit_one_out[0] = unit_one
    inverse_one_out[0] = inverse_one
    hidden = unit_one * gain_one + shift_one
    hidden_low = hidden.astype(BF)
    hidden_low_out[0] = hidden_low
    ready(4, 5)
    total = hidden + b_down
    for c in range(gelu_out.shape[2] // width):
        at = slice(c * width, (c + 1) * width)
        value, slope = gelu_and_slope(dot(hidden_low, w_up[:, at]) + vectors[8 + c : 9 + c, :])
        low = value.astype(BF)
        gelu_out[0, :, at] = low
        slope_out[0, :, at] = slope.astype(BF)
        total = total + dot(low, w_down[at, :])
    unit_two, inverse_two = normalize(total)
    unit_two_out[0] = unit_two
    inverse_two_out[0] = inverse_two
    act_held[...] = (unit_two * gain_two + shift_two).astype(BF)
    for k in range(pieces):
        act[k][0] = act_held[pl.ds(pl.multiple_of(src[k] * block, block), block), :]
    live = (lax.broadcasted_iota(jnp.int32, (span, 1), 0) < length).astype(F32)
    sums_out[0] = jnp.sum(unit_two * live, axis=0, keepdims=True)


def forward(lens, src, pieces, weights, vectors, passages, first, before, riders):
    count, block, width = pieces[0].shape
    n = len(pieces)
    span = block * n
    units = weights[4].shape[1]
    shapes = [
        ((span, width), BF), ((span, width), BF), ((span, width), BF), ((span, width), BF),
        ((span, width), BF), ((16, span), F32), ((span, width), F32), ((span, 1), F32),
        ((span, width), BF), ((span, units), BF), ((span, units), BF), ((span, width), F32),
        ((span, 1), F32), ((1, width), F32),
    ]
    outs = [jax.ShapeDtypeStruct((passages,) + s, t) for s, t in shapes]
    outs += [jax.ShapeDtypeStruct((passages, block, width), BF)] * n
    out_specs = [per_passage(o.shape[1:], first) for o in outs]
    kinds = len(outs)
    in_specs = [per_passage((block, width))] * n + [ANYWHERE] * 6 + [whole(vectors.shape)]
    operands = list(pieces) + list(weights) + [vectors]
    aliases = {}
    if before is not None:
        for i, value in enumerate(before):
            aliases[2 + len(operands)] = i
            operands.append(value)
            in_specs.append(ANYWHERE)
    aliases.update(alias(operands, in_specs, outs, out_specs, riders, 2))

    def kernel(*refs):
        forward_kernel(
            *refs, pieces=n, first=first, aliased=0 if before is None else kinds,
            riders=len(riders),
        )

    return pl.pallas_call(
        kernel,
        out_shape=outs,
        grid_spec=pltpu.PrefetchScalarGridSpec(
            num_scalar_prefetch=2,
            grid=(count,),
            in_specs=in_specs,
            out_specs=out_specs,
            scratch_shapes=[pltpu.VMEM(w.shape, BF) for w in weights]
            + [pltpu.VMEM((span, width), BF), pltpu.SemaphoreType.DMA((6,))],
        ),
        input_output_aliases=aliases,
        compiler_params=pltpu.CompilerParams(vmem_limit_bytes=VMEM_BYTES),
        cost_estimate=BRIEF,
    )(lens, src, *operands)


def second_norm_back(length, push, unit_two, inverse_two):
    live = lax.broadcasted_iota(jnp.int32, (unit_two.shape[0], 1), 0) < length
    return jnp.where(live, norm_back(push, unit_two, inverse_two), 0.0)


def hand_over(total, kept_hbm, sent_hbm, side, place, sems):
    half = total.shape[0] // 2
    own = pl.multiple_of(side * half, half)
    other = pl.multiple_of((1 - side) * half, half)
    copies = [
        pltpu.make_async_copy(total.at[pl.ds(at, half), :], out.at[pl.ds(place, half), :], sem)
        for at, out, sem in ((own, kept_hbm, sems.at[0]), (other, sent_hbm, sems.at[1]))
    ]
    for copy in copies:
        copy.start()
    for copy in copies:
        copy.wait()


def alias(operands, specs, outs, out_specs, values, offset):
    pairs = {}
    for value in values:
        pairs[offset + len(operands)] = len(outs)
        operands.append(value)
        specs.append(ANYWHERE)
        outs.append(jax.ShapeDtypeStruct(value.shape, value.dtype))
        out_specs.append(ANYWHERE)
    return pairs


def feed_kernel(lens, core, *refs, part, parts, place, filling, riders):
    refs = list(refs)
    take = lambda n: [refs.pop(0) for _ in range(n)]
    opening, closing = part == 0, part == parts - 1
    if opening:
        push, unit_two, inverse_two = take(3)
    else:
        grad_low_in, grad_hidden_in = take(2)
    if closing:
        unit_one, inverse_one, mixed, gain_one = take(4)
    gelu, slope, hidden_low, w_down, w_up = take(5)
    if closing:
        (w_out,) = take(1)
    take((2 if filling else 0) + riders)
    grad_hidden_out, low_out, up_bias, rows = take(4)
    kept_hbm, sent_hbm = take(2)
    take(riders)
    total, sems = take(2)
    step = pl.program_id(0)
    last = pl.num_programs(0) - 1
    units, width = w_down.shape

    @pl.when(step == 0)
    def _():
        total[...] = jnp.zeros_like(total)
        up_bias[...] = jnp.zeros_like(up_bias)
        rows[...] = jnp.zeros_like(rows)

    if opening:
        grad_hidden = second_norm_back(lens[step], push[0], unit_two[0], inverse_two[0])
        grad_low = grad_hidden.astype(BF)
        low_out[0] = grad_low
        rows[3:4, :] += jnp.sum(grad_low.astype(F32), axis=0, keepdims=True)
    else:
        grad_hidden = grad_hidden_in[0]
        grad_low = grad_low_in[0]
    up_low = (dot(grad_low, w_down[...], 1, 1) * slope[0].astype(F32)).astype(BF)
    total[:units, :] += dot(gelu[0], grad_low, 0, 0)
    up_bias[...] += jnp.sum(up_low.astype(F32), axis=0, keepdims=True)
    total[total.shape[0] - width :, :] += dot(hidden_low[0], up_low, 0, 0)
    grad_hidden = grad_hidden + dot(up_low, w_up[...], 1, 1)
    if closing:
        unit = unit_one[0]
        rows[0:1, :] += jnp.sum(grad_hidden * unit, axis=0, keepdims=True)
        rows[1:2, :] += jnp.sum(grad_hidden, axis=0, keepdims=True)
        grad_one = norm_back(grad_hidden * gain_one[...], unit, inverse_one[0])
        grad_hidden_out[0] = grad_one
        branch_low = grad_one.astype(BF)
        rows[2:3, :] += jnp.sum(branch_low.astype(F32), axis=0, keepdims=True)
        total[units : units + width, :] += dot(mixed[0], branch_low, 0, 0)
        low_out[0] = dot(branch_low, w_out[...], 1, 1).astype(BF)
    else:
        grad_hidden_out[0] = grad_hidden

    @pl.when(step == last)
    def _():
        hand_over(total, kept_hbm, sent_hbm, core[0], place, sems)


def feed_back(lens, core, row_operands, gelu, slope, hidden_low, w_down, w_up, w_out, part, parts,
              place, tall_all, filled, riders):
    opening, closing = part == 0, part == parts - 1
    passages, span, units = gelu.shape
    units //= parts
    width = w_down.shape[1]
    tall = 2 * units + (width if closing else 0)
    tile = per_passage((span, width))
    column = per_passage((span, 1))
    chunk = pl.BlockSpec((1, span, units), lambda i, *_: (i, 0, part))
    specs = [per_passage((1, width)), tile, column] if opening else [tile, tile]
    operands = list(row_operands)
    if closing:
        specs += [tile, column, tile, whole((1, width))]
    operands += [gelu, slope, hidden_low, w_down, w_up]
    specs += [
        chunk, chunk, tile,
        pl.BlockSpec((units, width), lambda i, *_: (part, 0)),
        pl.BlockSpec((width, units), lambda i, *_: (0, part)),
    ]
    if closing:
        operands.append(w_out)
        specs.append(whole((width, width)))
    like = lambda t: jax.ShapeDtypeStruct((passages, span, width), t)
    outs = [
        like(F32), like(BF), jax.ShapeDtypeStruct((1, units), F32),
        jax.ShapeDtypeStruct((8, width), F32),
    ]
    out_specs = [tile, tile, whole((1, units)), whole((8, width))]
    if filled is None:
        outs += [jax.ShapeDtypeStruct((tall_all, width), F32)] * 2
        out_specs += [ANYWHERE] * 2
        pairs = alias(operands, specs, outs, out_specs, riders, 2)
    else:
        pairs = alias(operands, specs, outs, out_specs, tuple(filled) + tuple(riders), 2)

    def kernel(*refs):
        feed_kernel(
            *refs, part=part, parts=parts, place=place, filling=filled is not None,
            riders=len(riders),
        )

    return pl.pallas_call(
        kernel,
        out_shape=outs,
        grid_spec=pltpu.PrefetchScalarGridSpec(
            num_scalar_prefetch=2,
            grid=(passages,),
            in_specs=specs,
            out_specs=out_specs,
            scratch_shapes=[pltpu.VMEM((tall, width), F32), pltpu.SemaphoreType.DMA((2,))],
        ),
        input_output_aliases=pairs,
        compiler_params=pltpu.CompilerParams(vmem_limit_bytes=VMEM_BYTES),
        cost_estimate=BRIEF,
    )(lens, core, *operands)


def attention_kernel(
    lens, src, core, *refs, pieces, final, part, first, opening, closing, filled, riders
):
    refs = list(refs)
    take = lambda n: [refs.pop(0) for _ in range(n)]
    x, q, k, v, lse, grad_mixed, grad_in = take(7)
    weights = take(3)
    if not opening:
        (total_in,) = take(1)
    take(filled + riders)
    out = take(pieces if final else 1)
    (bias,) = take(1)
    totals_out = take(2 if closing else 1)
    take(riders)
    total = take(1)[0]
    lows = take(3)
    tokens_low, sems = take(2)
    step = pl.program_id(0)
    last = pl.num_programs(0) - 1
    span, columns = q.shape[1:]
    width = x.shape[2]
    block = span // pieces
    head = width // HEADS
    pair = 2 * head
    scale = head ** -0.5
    if not opening:
        before = pltpu.make_async_copy(total_in, total, sems.at[0])

    @pl.when(step == 0)
    def _():
        if opening:
            total[...] = jnp.zeros_like(total)
        else:
            before.start()
        bias[...] = jnp.zeros_like(bias)

    key_mask = jnp.where(
        lax.broadcasted_iota(jnp.int32, (span, 1), 0) < lens[first + step], 0.0, MASKED
    ).astype(F32)
    query_low, key_low, value_low = lows
    for p in range(columns // pair):
        at = slice(p * pair, (p + 1) * pair)
        qp, kp, vp, gp = q[0, :, at], k[0, :, at], v[0, :, at], grad_mixed[0, :, at]
        gq = gk = gv = None
        for h in range(2):
            half = lane_half(pair, h).astype(BF)
            qm, gm, km = qp * half, gp * half, kp * half
            n = part * (columns // head) + 2 * p + h
            probs = jnp.exp((dot(kp, qm, 1, 1) + key_mask) - lse[0, n : n + 1, :])
            low = probs.astype(BF)
            grad_probs = dot(vp, gm, 1, 1)
            delta = jnp.sum(probs * grad_probs, axis=0, keepdims=True)
            scores = (probs * (grad_probs - delta)).astype(BF)
            tv = dot(low, gm)
            tk = dot(scores, qm)
            tq = dot(scores, km, 0, 0)
            gv = tv if gv is None else gv + tv
            gk = tk if gk is None else gk + tk
            gq = tq if gq is None else gq + tq
        query_low[:, at] = (gq * scale).astype(BF)
        key_low[:, at] = gk.astype(BF)
        value_low[:, at] = gv.astype(BF)

    if not opening:

        @pl.when(step == 0)
        def _():
            before.wait()

    grad = grad_in[0]
    for n, (low, weight) in enumerate(zip(lows, weights)):
        grad = grad + dot(low[...], weight[...], 1, 1)
        total[:, n * columns : (n + 1) * columns] += dot(x[0], low[...], 0, 0)
    bias[0:1, :] += jnp.sum(query_low[...].astype(F32), axis=0, keepdims=True)
    bias[1:2, :] += jnp.sum(value_low[...].astype(F32), axis=0, keepdims=True)
    if final:
        tokens_low[...] = grad.astype(BF)
        for n in range(pieces):
            out[n][0] = tokens_low[pl.ds(pl.multiple_of(src[n] * block, block), block), :]
    else:
        out[0][0] = grad

    @pl.when(step == last)
    def _():
        if closing:
            hand_over(total, *totals_out, core[0], 0, sems)
        else:
            after = pltpu.make_async_copy(total, totals_out[0], sems.at[1])
            after.start()
            after.wait()


def attention_back(lens, src, core, pieces, x, q, k, v, lse, grad_mixed, grad_in, weights, part,
                   parts, first, count, grad_first, total, closing, before, riders):
    passages, span, width = x.shape
    block = span // pieces
    columns = width // parts
    final = part == parts - 1
    tall = width

    def kernel(*refs):
        attention_kernel(
            *refs, pieces=pieces, final=final, part=part, first=first, opening=total is None,
            closing=closing, filled=len(before), riders=len(riders),
        )

    tile = per_passage((span, width), first)
    chunk = pl.BlockSpec((1, span, columns), lambda i, *_: (i + first, 0, part))
    if final:
        outs = [jax.ShapeDtypeStruct((passages, block, width), BF)] * pieces
        out_specs = [per_passage((block, width), first)] * pieces
    else:
        outs = [jax.ShapeDtypeStruct((count, span, width), F32)]
        out_specs = [per_passage((span, width))]
    outs.append(jax.ShapeDtypeStruct((2, columns), F32))
    out_specs.append(whole((2, columns)))
    if closing:
        outs += [jax.ShapeDtypeStruct((tall // 2, 3 * columns), F32)] * 2
        out_specs += [ANYWHERE] * 2
    else:
        outs.append(jax.ShapeDtypeStruct((tall, 3 * columns), F32))
        out_specs.append(ANYWHERE)
    operands = [x, q, k, v, lse, grad_mixed, grad_in, *weights]
    specs = [tile, chunk, chunk, chunk, per_passage(lse.shape[1:], first), chunk]
    specs.append(per_passage((span, width), grad_first))
    specs += [pl.BlockSpec((width, columns), lambda i, *_: (0, part))] * 3
    if total is not None:
        operands.append(total)
        specs.append(ANYWHERE)
    pairs = {}
    for i, value in enumerate(before):
        pairs[3 + len(operands)] = i
        operands.append(value)
        specs.append(ANYWHERE)
    pairs.update(alias(operands, specs, outs, out_specs, riders, 3))
    return pl.pallas_call(
        kernel,
        out_shape=outs,
        grid_spec=pltpu.PrefetchScalarGridSpec(
            num_scalar_prefetch=3,
            grid=(count,),
            in_specs=specs,
            out_specs=out_specs,
            scratch_shapes=[pltpu.VMEM((tall, 3 * columns), F32)]
            + [pltpu.VMEM((span, columns), BF)] * 3
            + [pltpu.VMEM((span, width), BF), pltpu.SemaphoreType.DMA((2,))],
        ),
        input_output_aliases=pairs,
        compiler_params=pltpu.CompilerParams(vmem_limit_bytes=VMEM_BYTES),
        cost_estimate=BRIEF,
    )(lens, src, core, *operands)


def tick(values):
    operands, specs, outs, out_specs = [], [], [], []
    pairs = alias(operands, specs, outs, out_specs, values, 0)
    return pl.pallas_call(
        lambda *refs: None,
        out_shape=outs,
        in_specs=specs,
        out_specs=out_specs,
        input_output_aliases=pairs,
        cost_estimate=TICK,
    )(*operands)


def flip(value, amount, axes, devices):
    return lax.ppermute(value, axes, [(i, i ^ amount) for i in range(devices)])


class Summing:
    def __init__(self, kept, sent, bits, short, me, devices, plan=(), extra=None):
        self.kept, self.sent, self.bits, self.short = kept, sent, list(bits), short
        self.me, self.devices, self.plan, self.extra = me, devices, list(plan), extra
        self.left = 0
        self.done = False

    def launch(self):
        bit = self.bits.pop(0)
        self.narrow = bit in self.short
        sent = self.sent.astype(BF) if self.narrow else self.sent
        if self.extra is not None:
            if self.narrow:
                high = lax.reduce_precision(self.extra, 8, 7)
                low = lax.reduce_precision(self.extra - high, 8, 7)
                self.extra = high + low
                sent = jnp.concatenate([sent, high.astype(BF), low.astype(BF)], axis=0)
            else:
                sent = jnp.concatenate([sent, self.extra], axis=0)
        self.came = flip(sent, 1 << bit, BOTH, self.devices)
        self.left = self.plan.pop(0) if self.plan else 1

    def land(self):
        self.left = 0
        rows = self.kept.shape[0]
        came = self.came.astype(F32)
        if self.extra is not None:
            n = self.extra.shape[0]
            more = came[rows : rows + n]
            if self.narrow:
                more = more + came[rows + n :]
            self.extra = self.extra + more
            came = came[:rows]
        value = self.kept + came
        if not self.bits:
            self.kept = value.astype(BF)
            self.done = True
            return
        side = (self.me >> self.bits[0]) & 1
        self.sent = lax.dynamic_slice_in_dim(value, (1 - side) * (rows // 2), rows // 2)
        self.kept = lax.dynamic_slice_in_dim(value, side * (rows // 2), rows // 2)


class Gathering:
    def __init__(self, value, bits, me, devices):
        self.kept, self.bits, self.me, self.devices = value, list(bits)[::-1], me, devices
        self.left = 0
        self.done = not self.bits

    def launch(self):
        self.bit = self.bits.pop(0)
        self.came = flip(self.kept, 1 << self.bit, BOTH, self.devices)
        self.left = 1

    def land(self):
        self.kept = jnp.where(
            ((self.me >> self.bit) & 1) == 0,
            jnp.concatenate([self.kept, self.came], axis=0),
            jnp.concatenate([self.came, self.kept], axis=0),
        )
        self.left = 0
        self.done = not self.bits


class Homing:
    def __init__(self, pieces, kind, seq_at, stretch):
        n = len(pieces)
        mine, block, width = pieces[0].shape
        self.kind, self.seq_at, self.stretch = kind, seq_at, stretch
        self.kept = jnp.zeros((n, mine, block, width), kind)
        self.waiting = [(k, pieces[k]) for k in (*range(2, n), 1)[: n - 1]]
        self.place(0, pieces[0])
        self.came = []
        self.left = 0
        self.done = False
        self.n = n

    def place(self, k, piece):
        self.kept = lax.dynamic_update_slice_in_dim(
            self.kept, piece.astype(self.kind)[None], self.seq_at ^ k, 0
        )

    def launch(self):
        take = max(1, (self.n - 1) // 3)
        self.came = [(k, flip(p, k, "seq", self.n)) for k, p in self.waiting[:take]]
        self.waiting = self.waiting[take:]
        self.left = self.stretch

    def land(self):
        for k, piece in self.came:
            self.place(k, piece)
        self.left = 0
        self.done = not self.waiting

    def whole(self):
        n, mine, block, width = self.kept.shape
        return self.kept.reshape(n * mine, block, width)


def in_order(every, bits):
    n = len(bits)
    width = every.shape[-1]
    every = every.reshape((2,) * n + (-1, width))
    every = every.transpose(tuple(n - 1 - b for b in bits) + (n, n + 1))
    return every.reshape(-1, width)


def local(
    tokens, sources, lengths, pairing, queries, w_query, b_query, w_key, w_value, b_value, w_out,
    b_out, gain_one, shift_one, w_up, b_up, w_down, second_feedforward_offset, gain_two, shift_two,
):
    documents, block, width = tokens.shape
    n_seq, n_dp = lax.axis_size("seq"), lax.axis_size("dp")
    devices = n_seq * n_dp
    seq_at, dp_at = lax.axis_index("seq"), lax.axis_index("dp")
    me = dp_at * n_seq + seq_at
    mine = documents // n_seq
    batch = documents * n_dp
    units = w_up.shape[1]
    src = seq_at ^ jnp.arange(n_seq, dtype=jnp.int32)
    lens = lax.dynamic_slice_in_dim(lengths, seq_at * mine, mine)

    def arriving(first, count, before):
        late = 0
        if before is not None:
            late = (before[-1][0, 0, 0] != before[-1][0, 0, 0]).astype(jnp.int32)
        pieces = []
        for k in range(n_seq):
            rows = lax.dynamic_slice_in_dim(tokens, (seq_at ^ k) * mine + first + late, count)
            pieces.append(rows if k == 0 else flip(rows, k, "seq", n_seq))
        return pieces

    weights = (w_query, w_key, w_value, w_out, w_up, w_down)
    row = lambda v: v[None, :]
    vectors = [b_query, b_value, b_out, gain_one, shift_one, second_feedforward_offset, gain_two,
               shift_two, b_up]
    vectors = jnp.concatenate(vectors).reshape(-1, width)
    saved = None
    first = 0
    pieces = None
    dp_hops = n_dp.bit_length() - 1
    hop = lambda value, bit: flip(value, 1 << bit, "dp", n_dp)
    spread = queries[None]
    done = min(1, dp_hops)
    if done:
        spread = jnp.concatenate([spread, hop(spread, 0)], axis=0)
    for count in (1, mine - 1):
        pieces = arriving(first, count, pieces)
        came = [hop(spread, done)] if done < dp_hops else []
        *saved, spread = forward(
            lens, src, pieces, weights, vectors, mine, first, saved, (spread,)
        )
        spread = jnp.concatenate([spread] + came, axis=0)
        done += len(came)
        first += count
    for bit in range(done, dp_hops):
        spread = jnp.concatenate([spread, hop(spread, bit)], axis=0)
    (x, q, k, v, mixed, lse, unit_one, inverse_one, hidden_low, gelu, slope, unit_two, inverse_two,
     unit_sums) = saved[:14]
    act = saved[14:]

    asked = jnp.concatenate(
        [lax.dynamic_index_in_dim(spread, dp_at ^ i, 0, False) for i in range(n_dp)], axis=0
    ).astype(F32)
    asked = asked * lax.rsqrt(jnp.sum(asked * asked, axis=-1, keepdims=True) + 1e-06)
    count = lens.astype(F32)[:, None]
    pooled = (unit_sums[:, 0, :] * gain_two + count * shift_two) / count
    pooled_inverse = lax.rsqrt(jnp.sum(pooled * pooled, axis=-1, keepdims=True) + 1e-06)
    pooled_unit = pooled * pooled_inverse
    own = jnp.dot(pooled_unit, asked.T, precision=EXACT) / TEMPERATURE
    scores = own[None]
    for bit in range(devices.bit_length() - 1):
        scores = jnp.concatenate([scores, flip(scores, 1 << bit, BOTH, devices)], axis=0)
    scores = scores.reshape(batch, batch)
    everyone = jnp.arange(batch, dtype=jnp.int32)
    order = ((me ^ jnp.arange(devices, dtype=jnp.int32))[:, None] * mine
             + jnp.arange(mine, dtype=jnp.int32)[None, :]).reshape(batch)
    pick = lambda index: jnp.sum(
        jnp.where(index[:, None] == everyone[None, :], sources[None, :], 0), axis=1
    )
    same = pick(order)[:, None] == pick(pairing)[None, :]
    match = order[:, None] == pairing[None, :]
    scores = jnp.where(same, scores, MASKED)
    top = jnp.max(scores, axis=0)
    log_total = top + jnp.log(jnp.sum(jnp.exp(scores - top), axis=0))
    chosen = jnp.sum(jnp.where(match, scores, 0.0), axis=0)
    loss = jnp.sum(log_total - chosen) / batch
    grad_scores = (jnp.exp(scores[:mine] - log_total) - match[:mine].astype(F32)) * (
        1.0 / batch / TEMPERATURE
    )
    grad_unit = jnp.dot(grad_scores, asked, precision=EXACT)
    grad_pooled = pooled_inverse * (
        grad_unit - pooled_unit * jnp.sum(grad_unit * pooled_unit, axis=-1, keepdims=True)
    )
    each = grad_pooled / count
    push = (each * gain_two)[:, None, :]
    grad_gain_two = jnp.sum(each * unit_sums[:, 0, :], axis=0)
    grad_shift_two = jnp.sum(grad_pooled, axis=0)

    seq_bits = n_seq.bit_length() - 1
    top_bit = devices.bit_length() - 1
    far_bits = tuple(range(seq_bits + 1, top_bit))
    bits = (0, seq_bits) + tuple(range(1, seq_bits)) + far_bits
    bits_b = tuple(range(top_bit))
    short = range(1, seq_bits + 1)
    core = (me & 1)[None]
    feed_parts = units // width
    heads_parts = 1
    feed = (gelu, slope, hidden_low, w_down, w_up, w_out)
    flying = []

    def begin(kept, sent, bits, *plan, extra=None):
        one = Summing(kept, sent, bits, short, me, devices, plan, extra)
        flying.append(one)
        return one

    def riding():
        for one in flying:
            if not one.left and not one.done:
                one.launch()
        return tuple(one.kept for one in flying)

    def landing(kept):
        for one, value in zip(list(flying), kept):
            one.kept = value
            if one.done:
                flying.remove(one)
                continue
            one.left -= 1
            if not one.left:
                one.land()

    up_biases = []
    operands = (push, unit_two, inverse_two)
    chunks = []
    for part in range(feed_parts):
        closing = part == feed_parts - 1
        second = part % 2
        if closing:
            operands = operands + (unit_one, inverse_one, mixed, row(gain_one))
        riders = riding()
        if part == 0:
            riders += tuple(act)
        tall_all = 2 * width + (width // 2 if part >= feed_parts - 2 else 0)
        grad_hidden, low, up_bias, rows, kept, sent, *landed = feed_back(
            lens, core, operands, *feed, part, feed_parts, second * width, tall_all,
            (kept, sent) if second else None, riders,
        )
        if part == 0:
            activations = Homing(landed, BF, seq_at, 1)
            activations.waiting.sort()
            flying.append(activations)
        else:
            landing(landed)
        up_biases.append(up_bias)
        if part == 0:
            rows_a, grad_low = rows, low
        operands = (grad_low, grad_hidden)
        if second:
            chunks.append(begin(kept, sent, *((bits_b, 1, 2) if closing else (bits,))))
    grad_one, grad_mixed, rows_b = grad_hidden, low, rows
    biases = []
    grad_in = grad_one
    for part in range(heads_parts):
        riders = riding()
        outs = attention_back(
            lens, src, core, n_seq, x, q, k, v, lse, grad_mixed, grad_in,
            (w_query, w_key, w_value), part, heads_parts, 0, mine, 0, None, True, (), riders,
        )
        n = n_seq if part == heads_parts - 1 else 1
        landing(outs[n + 3 :])
        grad_in = outs[0]
        biases.append(outs[n])
        kept, sent = outs[n + 1 : n + 3]
        extra = None
        if part == heads_parts - 1:
            extra = jnp.concatenate(
                [
                    jnp.concatenate(biases, axis=1), rows_b[0:3], rows_a[3:4],
                    row(grad_gain_two), row(grad_shift_two),
                    jnp.concatenate(up_biases, axis=1).reshape(feed_parts, width),
                    jnp.zeros((-(8 + feed_parts) % 16, width), F32),
                ],
                axis=0,
            )
        extra = jnp.concatenate([extra, jnp.zeros((-len(extra) % 3, width), F32)], axis=0)
        chunks.append(begin(kept, sent, bits, extra=extra.reshape(-1, 3 * width)))
    homes = Homing(outs[:n_seq], F32, seq_at, 2)
    flying.append(homes)
    first, second, heads = chunks
    feed = attention = None
    while flying:
        if first.done and second.done and feed is None:
            feed = jnp.concatenate([first.kept, second.kept], axis=0)
            feed = lax.all_gather(feed, BOTH, axis=0)
        if heads.done and attention is None:
            attention = Gathering(heads.kept, bits, me, devices)
            flying.append(attention)
        flying = [one for one in flying if not one.done]
        if flying:
            landing(tick(riding()))
    small = heads.extra.reshape(-1, width)
    attention = attention.kept
    cut = first.kept.shape[0]
    all_a, all_b = in_order(feed[:, :cut], bits), in_order(feed[:, cut:], bits_b)
    activations, grad_tokens = activations.whole(), homes.whole()
    grads = [attention[:, n * width : (n + 1) * width].astype(F32) for n in range(3)]
    two = 2 * width
    half = two + width // 2
    again = half + width
    grad_down = jnp.concatenate([all_a[:two], all_b[:two]], axis=0).astype(F32)
    grad_out = jnp.concatenate(
        [all_b[two:half], all_b[again : again + width // 2]], axis=0
    ).astype(F32)
    grad_up = jnp.concatenate(
        [all_a[two : two + width], all_a[two + width :], all_b[half:again],
         all_b[again + width // 2 :]],
        axis=1,
    ).astype(F32)
    return (
        loss,
        activations,
        grad_tokens,
        grads[0],
        small[0],
        grads[1],
        grads[2],
        small[1],
        grad_out,
        small[4],
        small[2],
        small[3],
        grad_up,
        small[8 : 8 + feed_parts].reshape(units),
        grad_down,
        small[5],
        small[6],
        small[7],
    )


def solution(mesh):
    in_specs = (P("dp", "seq", None), P(), P("dp"), P(), P("dp", None)) + (P(),) * 15
    out_specs = (P(), P("dp", "seq", None), P("dp", "seq", None)) + (P(),) * 15
    return jax.shard_map(local, mesh=mesh, in_specs=in_specs, out_specs=out_specs, check_vma=False)
```

time: 1700 us -> 659 us (0.39)
  blocking collectives: 575 us -> 0 us
  matrix products: 373 us -> 0.99 us
  waiting for transfers between devices: 471 us -> 205 us
  Pallas kernels: 0 us -> 249 us
  local copies, waits for them, and re-layouts: 128 us -> 64.6 us
  other arithmetic: 131 us -> 72.1 us
  starting transfers between devices: 0.42 us -> 38.1 us
    unnamed x2 -> x0, blocking collectives: 500 us -> none
    dot_general x25 -> x2, matrix products: 347 us -> 0.99 us  [the longest x1 0.5 us: local(): grad_unit = jnp.dot(grad_scores, asked, precision=EXACT)]
    all_gather x8 -> x1, waiting for transfers between devices: 323 us -> 0.01 us  [local(): feed = lax.all_gather(feed, BOTH, axis=0)]
    pallas_call x0 -> x17, Pallas kernels: none -> 249 us  [the longest x2 100 us: forward(): pl.pallas_call(kernel, out_shape=outs, grid_spec=pltpu.PrefetchScalarGrid...]
    ppermute x0 -> x40, waiting for transfers between devices: none -> 205 us  [flip(): return lax.ppermute(value, axes, [(i, i ^ amount) for i in range(devices)])]
    reduce_scatter x2 -> x0, waiting for transfers between devices: 147 us -> none  [the longest x1 147 us: local(): lax.psum_scatter(key_terms, 'seq', scatter_dimension=1, tiled=True)]
    convert_element_type x6 -> x13, other arithmetic: 106 us -> 21.7 us  [the longest x1 4.48 us: local(): grad_down = jnp.concatenate([all_a[:two], all_b[:two]], axis=0).astype(F32)]
    all_gather x2 -> x0, blocking collectives: 64.8 us -> none  [the longest x1 33.3 us: local(): lax.all_gather(query_rows, 'dp', axis=0, tiled=True)]
  transfers between devices with their start and end apart: 10 -> 41, of which waited for: 8 -> 17; matrix products, arithmetic and copies ran while one was open for 20% -> 16% of each run, Pallas kernels for 0% -> 24%
where the time goes in v1:
time: 659 us; the launch traced here: 648 us
  Pallas kernels  249 us (38%)
  waiting for transfers between devices  205 us (31%)
  other arithmetic  72.1 us (11%)
  local copies, waits for them, and re-layouts  64.6 us (10%)
  starting transfers between devices  38.1 us (6%)
  between operations  18.5 us (3%)
    ppermute x40, waiting for transfers between devices, flip(): return lax.ppermute(value, axes, [(i, i ^ amount) for i in range(devices)])  205 us
    pallas_call x2, Pallas kernels, forward(): pl.pallas_call(kernel, out_shape=outs, grid_spec=pltpu.PrefetchScalarGrid...  100 us
    pallas_call x4, Pallas kernels, feed_back(): pl.pallas_call(kernel, out_shape=outs, grid_spec=pltpu.PrefetchScalarGrid...  85.9 us
    pallas_call x1, Pallas kernels, attention_back(): pl.pallas_call(kernel, out_shape=outs, grid_spec=pltpu.PrefetchScalarGrid...  62.4 us
    ppermute x40, starting transfers between devices, flip(): return lax.ppermute(value, axes, [(i, i ^ amount) for i in range(devices)])  38.1 us
    add x12, other arithmetic, land(): value = self.kept + came  20.5 us
    unnamed x100, local copies, waits for them, and re-layouts  14.3 us
  transfers between devices with their start and end apart: 41, of which 17 were waited for; matrix products, arithmetic and copies ran while one was open for 16% of the time, Pallas kernels for 24%

profile of v1, /device:TPU:0, one launch (start us, length us, event | category | flops | bytes accessed | tf_op | source)
XLA Modules:
  0.0 647.7 jit_solution(16819061491922145970)
XLA Ops:
  31.1 25.5 %shard_map.331 = (bf16[4,512,768]{2,1,0:T(8,128)(2,1)}, bf16[4,512,768]{2,1,0:T(8,128)(2,1)}, bf16[4,512,768]{2,1,0:T(8,128)(2,1)}, bf16[4,512,768]{2,1,0:T(8,12...) custom-call(s32[4]{0:T(128)} %get-tuple-element.232.refs_0_, ...), custom_call_target="tpu_custom_call", output_to_operand_aliasing={{18}: (13, {})} | custom-call | flops 70000001024 | bytes 1000000 | tf_op jit(solution)/shard_map/pallas_call | solution.py:194
  60.1 5.3 collective-permute-done.8
  66.6 74.7 %shard_map.332 = (bf16[4,512,768]{2,1,0:T(8,128)(2,1)}, bf16[4,512,768]{2,1,0:T(8,128)(2,1)}, bf16[4,512,768]{2,1,0:T(8,128)(2,1)}, bf16[4,512,768]{2,1,0:T(8,12...) custom-call(s32[4]{0:T(128)} %get-tuple-element.232.refs_0_, ...), custom_call_target="tpu_custom_call", output_to_operand_aliasing={{0}: (13, {}), {1}: (14, {}), {2}: (15, {}), {3}: (16, {}),... | custom-call | flops 70000001024 | bytes 1000000 | tf_op jit(solution)/shard_map/pallas_call | solution.py:194
  164.0 19.5 %shard_map.333 = (f32[4,512,768]{2,1,0:T(8,128)}, bf16[4,512,768]{2,1,0:T(8,128)(2,1)}, f32[1,768]{1,0:T(1,128)}, f32[8,768]{1,0:T(8,128)}, f32[1536,768]{1,0:T(...) custom-call(s32[4]{0:T(128)} %get-tuple-element.232.refs_0_, ...), custom_call_target="tpu_custom_call", output_to_operand_aliasing={{6}: (10, {}), {7}: (11, {}), {8}: (12, {}), {9}: (13, {})} | custom-call | flops 70000001024 | bytes 1000000 | tf_op jit(solution)/shard_map/pallas_call | solution.py:342
  186.4 19.2 %shard_map.334 = (f32[4,512,768]{2,1,0:T(8,128)}, bf16[4,512,768]{2,1,0:T(8,128)(2,1)}, f32[1,768]{1,0:T(1,128)}, f32[8,768]{1,0:T(8,128)}, f32[1536,768]{1,0:T(...) custom-call(s32[4]{0:T(128)} %get-tuple-element.232.refs_0_, ...), custom_call_target="tpu_custom_call", output_to_operand_aliasing={{4}: (9, {}), {5}: (10, {}), {6}: (11, {})} | custom-call | flops 70000001024 | bytes 1000000 | tf_op jit(solution)/shard_map/pallas_call | solution.py:342
  212.1 19.1 %shard_map.335 = (f32[4,512,768]{2,1,0:T(8,128)}, bf16[4,512,768]{2,1,0:T(8,128)(2,1)}, f32[1,768]{1,0:T(1,128)}, f32[8,768]{1,0:T(8,128)}, f32[1920,768]{1,0:T(...) custom-call(s32[4]{0:T(128)} %get-tuple-element.232.refs_0_, ...), custom_call_target="tpu_custom_call", output_to_operand_aliasing={{6}: (9, {}), {7}: (10, {})} | custom-call | flops 70000001024 | bytes 1000000 | tf_op jit(solution)/shard_map/pallas_call | solution.py:342
  232.2 4.4 add.324
  238.9 28.0 %shard_map.336 = (f32[4,512,768]{2,1,0:T(8,128)}, bf16[4,512,768]{2,1,0:T(8,128)(2,1)}, f32[1,768]{1,0:T(1,128)}, f32[8,768]{1,0:T(8,128)}, f32[1920,768]{1,0:T(...) custom-call(s32[4]{0:T(128)} %get-tuple-element.232.refs_0_, ...), custom_call_target="tpu_custom_call", output_to_operand_aliasing={{4}: (14, {}), {5}: (15, {}), {6}: (16, {}), {7}: (17, {})} | custom-call | flops 70000001024 | bytes 1000000 | tf_op jit(solution)/shard_map/pallas_call | solution.py:342
  274.1 62.4 %shard_map.337 = (bf16[4,128,768]{2,1,0:T(8,128)(2,1)}, bf16[4,128,768]{2,1,0:T(8,128)(2,1)}, bf16[4,128,768]{2,1,0:T(8,128)(2,1)}, bf16[4,128,768]{2,1,0:T(8,12...) custom-call(s32[4]{0:T(128)} %get-tuple-element.232.refs_0_, ...), custom_call_target="tpu_custom_call", output_to_operand_aliasing={{7}: (13, {}), {8}: (14, {}), {9}: (15, {})} | custom-call | flops 70000001024 | bytes 1000000 | tf_op jit(solution)/shard_map/pallas_call | solution.py:493
  337.4 4.1 pad_maximum_fusion
  343.6 3.9 broadcast_in_dim.128
  348.7 8.7 %collective-permute-done.19 = bf16[384,768]{1,0:T(8,128)(2,1)S(1)} collective-permute-done((bf16[384,768]{1,0:T(8,128)(2,1)S(1)}, bf16[384,768]{1,0:T(8,128)(2,1)S(1)}, u32[]{:S(2)}, u32[]{:S(2)}) %collective-permute-start.19) | collective-permute-done | bytes 589856 | tf_op jit(solution)/shard_map/ppermute | solution.py:525
  385.8 9.4 %collective-permute-done.24 = bf16[204,2304]{1,0:T(8,128)(2,1)} collective-permute-done((bf16[204,2304]{1,0:T(8,128)(2,1)}, bf16[204,2304]{1,0:T(8,128)(2,1)}, u32[]{:S(2)}, u32[]{:S(2)}) %collective-permute-start.24) | collective-permute-done | bytes 940064 | tf_op jit(solution)/shard_map/ppermute | solution.py:525
  403.4 48.8 %collective-permute-done.27 = bf16[108,2304]{1,0:T(8,128)(2,1)S(1)} collective-permute-done((bf16[108,2304]{1,0:T(8,128)(2,1)S(1)}, bf16[108,2304]{1,0:T(8,128)(2,1)S(1)}, u32[]{:S(2)}, u32[]{:S(2)}) %collective-permute-start.27) | collective-permute-done | bytes 497696 | tf_op jit(solution)/shard_map/ppermute | solution.py:525
  460.0 11.7 %collective-permute-done.26 = bf16[480,768]{1,0:T(8,128)(2,1)S(1)} collective-permute-done((bf16[480,768]{1,0:T(8,128)(2,1)S(1)}, bf16[480,768]{1,0:T(8,128)(2,1)S(1)}, u32[]{:S(2)}, u32[]{:S(2)}) %collective-permute-start.26) | collective-permute-done | bytes 737312 | tf_op jit(solution)/shard_map/ppermute | solution.py:525
  476.7 11.5 %collective-permute-done.28 = f32[240,768]{1,0:T(8,128)S(1)} collective-permute-done((f32[240,768]{1,0:T(8,128)S(1)}, f32[240,768]{1,0:T(8,128)S(1)}, u32[]{:S(2)}, u32[]{:S(2)}) %collective-permute-start.28) | collective-permute-done | bytes 737312 | tf_op jit(solution)/shard_map/ppermute | solution.py:525
  496.1 9.5 %collective-permute-done.39 = f32[120,768]{1,0:T(8,128)S(1)} collective-permute-done((f32[120,768]{1,0:T(8,128)S(1)}, f32[120,768]{1,0:T(8,128)S(1)}, u32[]{:S(2)}, u32[]{:S(2)}) %collective-permute-start.39) | collective-permute-done | bytes 368672 | tf_op jit(solution)/shard_map/ppermute | solution.py:525
  508.4 21.7 %collective-permute-done.31 = f32[30,2304]{1,0:T(8,128)S(1)} collective-permute-done((f32[30,2304]{1,0:T(8,128)S(1)}, f32[30,2304]{1,0:T(8,128)S(1)}, u32[]{:S(2)}, u32[]{:S(2)}) %collective-permute-start.31) | collective-permute-done | bytes 276512 | tf_op jit(solution)/shard_map/ppermute | solution.py:525
  531.3 6.0 collective-permute-done.33
  538.5 15.7 %collective-permute-done.34 = bf16[48,2304]{1,0:T(8,128)(2,1)S(1)} collective-permute-done((bf16[48,2304]{1,0:T(8,128)(2,1)S(1)}, bf16[48,2304]{1,0:T(8,128)(2,1)S(1)}, u32[]{:S(2)}, u32[]{:S(2)}) %collective-permute-start.34) | collective-permute-done | bytes 221216 | tf_op jit(solution)/shard_map/ppermute | solution.py:525
  556.8 12.5 %collective-permute-done.35 = bf16[96,2304]{1,0:T(8,128)(2,1)S(1)} collective-permute-done((bf16[96,2304]{1,0:T(8,128)(2,1)S(1)}, bf16[96,2304]{1,0:T(8,128)(2,1)S(1)}, u32[]{:S(2)}, u32[]{:S(2)}) %collective-permute-start.35) | collective-permute-done | bytes 442400 | tf_op jit(solution)/shard_map/ppermute | solution.py:525
  572.2 31.4 %collective-permute-done.36 = bf16[192,2304]{1,0:T(8,128)(2,1)S(1)} collective-permute-done((bf16[192,2304]{1,0:T(8,128)(2,1)S(1)}, bf16[192,2304]{1,0:T(8,128)(2,1)S(1)}, u32[]{:S(2)}, u32[]{:S(2)}) %collective-permute-start.36) | collective-permute-done | bytes 884768 | tf_op jit(solution)/shard_map/ppermute | solution.py:525
  628.9 4.5 maximum_convert_fusion.1
  634.9 4.3 maximum_convert_fusion
  (300 shorter events, 167.4 us)
Async XLA Ops:
  7.2 614.4 %all-gather.3.cloned.1.call-start = ((), (), s32[]{:S(2)}) async-start(), calls=%async_computation | async-start | bytes 10948608 | tf_op jit(solution)/shard_map/all_gather | solution.py:822
  11.6 19.5 %collective-permute-start.4 = (bf16[1,128,768]{2,1,0:T(8,128)(2,1)S(1)}, bf16[1,128,768]{2,1,0:T(8,128)(2,1)}, u32[]{:S(2)}, u32[]{:S(2)}) collective-permute-start(bf16[1,128,768]{2,1,0:T(8,128)(2,1)S(1)} %get-tuple-element.249), channel_id=1, source_target_pairs={{0,1},{1,0},{2,3},{3,2},{4,5},{5,4},{6,7},{7,6},{8,9},{9,8},{10,11... | collective-permute-start | bytes 589832 | tf_op jit(solution)/shard_map/ppermute | solution.py:525
  12.3 18.8 %collective-permute-start.5 = (bf16[1,128,768]{2,1,0:T(8,128)(2,1)S(1)}, bf16[1,128,768]{2,1,0:T(8,128)(2,1)}, u32[]{:S(2)}, u32[]{:S(2)}) collective-permute-start(bf16[1,128,768]{2,1,0:T(8,128)(2,1)S(1)} %get-tuple-element.246), channel_id=1, source_target_pairs={{0,2},{1,3},{2,0},{3,1},{4,6},{5,7},{6,4},{7,5},{8,10},{9,11},{10,... | collective-permute-start | bytes 589832 | tf_op jit(solution)/shard_map/ppermute | solution.py:525
  29.2 36.1 %collective-permute-start.1 = (bf16[3,128,768]{2,1,0:T(8,128)(2,1)S(1)}, bf16[3,128,768]{2,1,0:T(8,128)(2,1)S(1)}, u32[]{:S(2)}, u32[]{:S(2)}) collective-permute-start(bf16[3,128,768]{2,1,0:T(8,128)(2,1)S(1)} %get-tuple-element.252), channel_id=1, source_target_pairs={{0,1},{1,0},{2,3},{3,2},{4,5},{5,4},{6,7},{7,6},{8,9},{9,8},{10,11... | collective-permute-start | bytes 1769480 | tf_op jit(solution)/shard_map/ppermute | solution.py:525
  29.2 36.1 %collective-permute-start.2 = (bf16[3,128,768]{2,1,0:T(8,128)(2,1)S(1)}, bf16[3,128,768]{2,1,0:T(8,128)(2,1)S(1)}, u32[]{:S(2)}, u32[]{:S(2)}) collective-permute-start(bf16[3,128,768]{2,1,0:T(8,128)(2,1)S(1)} %get-tuple-element.251), channel_id=1, source_target_pairs={{0,2},{1,3},{2,0},{3,1},{4,6},{5,7},{6,4},{7,5},{8,10},{9,11},{10,... | collective-permute-start | bytes 1769480 | tf_op jit(solution)/shard_map/ppermute | solution.py:525
  30.7 34.6 %collective-permute-start.3 = (bf16[3,128,768]{2,1,0:T(8,128)(2,1)S(1)}, bf16[3,128,768]{2,1,0:T(8,128)(2,1)S(1)}, u32[]{:S(2)}, u32[]{:S(2)}) collective-permute-start(bf16[3,128,768]{2,1,0:T(8,128)(2,1)S(1)} %get-tuple-element.250), channel_id=1, source_target_pairs={{0,3},{1,2},{2,1},{3,0},{4,7},{5,6},{6,5},{7,4},{8,11},{9,10},{10,... | collective-permute-start | bytes 1769480 | tf_op jit(solution)/shard_map/ppermute | solution.py:525
  183.6 26.5 %collective-permute-start.14 = (bf16[4,128,768]{2,1,0:T(8,128)(2,1)}, bf16[4,128,768]{2,1,0:T(8,128)(2,1)}, u32[]{:S(2)}, u32[]{:S(2)}) collective-permute-start(bf16[4,128,768]{2,1,0:T(8,128)(2,1)} %get-tuple-element.156), channel_id=1, source_target_pairs={{0,1},{1,0},{2,3},{3,2},{4,5},{5,4},{6,7},{7,6},{8,9},{9,8},{10,11... | collective-permute-start | bytes 2359304 | tf_op jit(solution)/shard_map/ppermute | solution.py:525
  205.6 26.6 %collective-permute-start.16 = (f32[1536,768]{1,0:T(8,128)}, f32[1536,768]{1,0:T(8,128)}, u32[]{:S(2)}, u32[]{:S(2)}) collective-permute-start(f32[1536,768]{1,0:T(8,128)} %get-tuple-element.167), channel_id=1, source_target_pairs={{0,1},{1,0},{2,3},{3,2},{4,5},{5,4},{6,7},{7,6},{8,9},{9,8},{10,11... | collective-permute-start | bytes 14155784 | tf_op jit(solution)/shard_map/ppermute | solution.py:525
  205.7 25.6 %collective-permute-start.15 = (bf16[4,128,768]{2,1,0:T(8,128)(2,1)}, bf16[4,128,768]{2,1,0:T(8,128)(2,1)S(1)}, u32[]{:S(2)}, u32[]{:S(2)}) collective-permute-start(bf16[4,128,768]{2,1,0:T(8,128)(2,1)} %get-tuple-element.165), channel_id=1, source_target_pairs={{0,2},{1,3},{2,0},{3,1},{4,6},{5,7},{6,4},{7,5},{8,10},{9,11},{10,... | collective-permute-start | bytes 2359304 | tf_op jit(solution)/shard_map/ppermute | solution.py:525
  207.3 61.8 %collective-permute-start.17 = (bf16[4,128,768]{2,1,0:T(8,128)(2,1)}, bf16[4,128,768]{2,1,0:T(8,128)(2,1)}, u32[]{:S(2)}, u32[]{:S(2)}) collective-permute-start(bf16[4,128,768]{2,1,0:T(8,128)(2,1)} %get-tuple-element.171), channel_id=1, source_target_pairs={{0,3},{1,2},{2,1},{3,0},{4,7},{5,6},{6,5},{7,4},{8,11},{9,10},{10,... | collective-permute-start | bytes 2359304 | tf_op jit(solution)/shard_map/ppermute | solution.py:525
  238.3 32.8 %collective-permute-start.18 = (bf16[768,768]{1,0:T(8,128)(2,1)S(1)}, bf16[768,768]{1,0:T(8,128)(2,1)S(1)}, u32[]{:S(2)}, u32[]{:S(2)}) collective-permute-start(bf16[768,768]{1,0:T(8,128)(2,1)S(1)} %dynamic-slice_convert_fusion.1), channel_id=1, source_target_pairs={{0,4},{1,5},{2,6},{3,7},{4,0},{5,1},{6,2},{7,3},{8,12},{9,13},{10,... | collective-permute-start | bytes 3538952 | tf_op jit(solution)/shard_map/ppermute | solution.py:525
  269.0 91.4 %collective-permute-start.20 = (f32[1920,768]{1,0:T(8,128)}, f32[1920,768]{1,0:T(8,128)}, u32[]{:S(2)}, u32[]{:S(2)}) collective-permute-start(f32[1920,768]{1,0:T(8,128)} %get-tuple-element.177), channel_id=1, source_target_pairs={{0,1},{1,0},{2,3},{3,2},{4,5},{5,4},{6,7},{7,6},{8,9},{9,8},{10,11... | collective-permute-start | bytes 17694728 | tf_op jit(solution)/shard_map/ppermute | solution.py:525
  341.5 17.3 %collective-permute-start.22 = (f32[390,2304]{1,0:T(8,128)}, f32[390,2304]{1,0:T(8,128)}, u32[]{:S(2)}, u32[]{:S(2)}) collective-permute-start(f32[390,2304]{1,0:T(8,128)} %pad_maximum_fusion), channel_id=1, source_target_pairs={{0,1},{1,0},{2,3},{3,2},{4,5},{5,4},{6,7},{7,6},{8,9},{9,8},{10,11... | collective-permute-start | bytes 10782728 | tf_op jit(solution)/shard_map/ppermute | solution.py:525
  358.6 17.2 %collective-permute-start.21 = (f32[192,768]{1,0:T(8,128)}, f32[192,768]{1,0:T(8,128)}, u32[]{:S(2)}, u32[]{:S(2)}) collective-permute-start(f32[192,768]{1,0:T(8,128)} %get-tuple-element.256), channel_id=1, source_target_pairs={{0,8},{1,9},{2,10},{3,11},{4,12},{5,13},{6,14},{7,15},{8,0},{9,1},... | collective-permute-start | bytes 1769480 | tf_op jit(solution)/shard_map/ppermute | solution.py:525
  372.8 22.5 %collective-permute-start.24 = (bf16[204,2304]{1,0:T(8,128)(2,1)}, bf16[204,2304]{1,0:T(8,128)(2,1)}, u32[]{:S(2)}, u32[]{:S(2)}) collective-permute-start(bf16[204,2304]{1,0:T(8,128)(2,1)} %pad_maximum_fusion.1), channel_id=1, source_target_pairs={{0,4},{1,5},{2,6},{3,7},{4,0},{5,1},{6,2},{7,3},{8,12},{9,13},{10,... | collective-permute-start | bytes 2820104 | tf_op jit(solution)/shard_map/ppermute | solution.py:525
  374.3 25.8 %collective-permute-start.25 = (bf16[4,128,768]{2,1,0:T(8,128)(2,1)}, bf16[4,128,768]{2,1,0:T(8,128)(2,1)}, u32[]{:S(2)}, u32[]{:S(2)}) collective-permute-start(bf16[4,128,768]{2,1,0:T(8,128)(2,1)} %get-tuple-element.195), channel_id=1, source_target_pairs={{0,2},{1,3},{2,0},{3,1},{4,6},{5,7},{6,4},{7,5},{8,10},{9,11},{10,... | collective-permute-start | bytes 2359304 | tf_op jit(solution)/shard_map/ppermute | solution.py:525
  375.7 117.2 %collective-permute-start.30 = (bf16[4,128,768]{2,1,0:T(8,128)(2,1)}, bf16[4,128,768]{2,1,0:T(8,128)(2,1)}, u32[]{:S(2)}, u32[]{:S(2)}) collective-permute-start(bf16[4,128,768]{2,1,0:T(8,128)(2,1)} %get-tuple-element.202), channel_id=1, source_target_pairs={{0,3},{1,2},{2,1},{3,0},{4,7},{5,6},{6,5},{7,4},{8,11},{9,10},{10,... | collective-permute-start | bytes 2359304 | tf_op jit(solution)/shard_map/ppermute | solution.py:525
  377.9 96.5 %collective-permute-start.38 = (f32[96,768]{1,0:T(8,128)}, f32[96,768]{1,0:T(8,128)}, u32[]{:S(2)}, u32[]{:S(2)}) collective-permute-start(f32[96,768]{1,0:T(8,128)} %get-tuple-element.262), channel_id=1, source_target_pairs={{0,16},{1,17},{2,18},{3,19},{4,20},{5,21},{6,22},{7,23},{8,24},{9,... | collective-permute-start | bytes 884744 | tf_op jit(solution)/shard_map/ppermute | solution.py:525
  383.9 68.3 %collective-permute-start.23 = (bf16[960,768]{1,0:T(8,128)(2,1)}, bf16[960,768]{1,0:T(8,128)(2,1)}, u32[]{:S(2)}, u32[]{:S(2)}) collective-permute-start(bf16[960,768]{1,0:T(8,128)(2,1)} %dynamic-slice_convert_fusion), channel_id=1, source_target_pairs={{0,2},{1,3},{2,0},{3,1},{4,6},{5,7},{6,4},{7,5},{8,10},{9,11},{10,... | collective-permute-start | bytes 4423688 | tf_op jit(solution)/shard_map/ppermute | solution.py:525
  398.5 53.7 %collective-permute-start.27 = (bf16[108,2304]{1,0:T(8,128)(2,1)S(1)}, bf16[108,2304]{1,0:T(8,128)(2,1)S(1)}, u32[]{:S(2)}, u32[]{:S(2)}) collective-permute-start(bf16[108,2304]{1,0:T(8,128)(2,1)S(1)} %pad_maximum_fusion.2), channel_id=1, source_target_pairs={{0,2},{1,3},{2,0},{3,1},{4,6},{5,7},{6,4},{7,5},{8,10},{9,11},{10,... | collective-permute-start | bytes 1493000 | tf_op jit(solution)/shard_map/ppermute | solution.py:525
  455.3 16.3 %collective-permute-start.26 = (bf16[480,768]{1,0:T(8,128)(2,1)S(1)}, bf16[480,768]{1,0:T(8,128)(2,1)S(1)}, u32[]{:S(2)}, u32[]{:S(2)}) collective-permute-start(bf16[480,768]{1,0:T(8,128)(2,1)S(1)} %dynamic-slice_convert_fusion.3), channel_id=1, source_target_pairs={{0,4},{1,5},{2,6},{3,7},{4,0},{5,1},{6,2},{7,3},{8,12},{9,13},{10,... | collective-permute-start | bytes 2211848 | tf_op jit(solution)/shard_map/ppermute | solution.py:525
  458.2 17.3 %collective-permute-start.29 = (f32[54,2304]{1,0:T(8,128)S(1)}, f32[54,2304]{1,0:T(8,128)}, u32[]{:S(2)}, u32[]{:S(2)}) collective-permute-start(f32[54,2304]{1,0:T(8,128)S(1)} %pad_maximum_fusion.3), channel_id=1, source_target_pairs={{0,8},{1,9},{2,10},{3,11},{4,12},{5,13},{6,14},{7,15},{8,0},{9,1},... | collective-permute-start | bytes 1493000 | tf_op jit(solution)/shard_map/ppermute | solution.py:525
  508.3 21.8 %collective-permute-start.31 = (f32[30,2304]{1,0:T(8,128)S(1)}, f32[30,2304]{1,0:T(8,128)S(1)}, u32[]{:S(2)}, u32[]{:S(2)}) collective-permute-start(f32[30,2304]{1,0:T(8,128)S(1)} %pad_maximum_fusion.5), channel_id=1, source_target_pairs={{0,16},{1,17},{2,18},{3,19},{4,20},{5,21},{6,22},{7,23},{8,24},{9,... | collective-permute-start | bytes 829448 | tf_op jit(solution)/shard_map/ppermute | solution.py:525
  570.7 32.9 %collective-permute-start.36 = (bf16[192,2304]{1,0:T(8,128)(2,1)S(1)}, bf16[192,2304]{1,0:T(8,128)(2,1)S(1)}, u32[]{:S(2)}, u32[]{:S(2)}) collective-permute-start(bf16[192,2304]{1,0:T(8,128)(2,1)S(1)} %maximum_select_fusion.2.refs_0_), channel_id=1, source_target_pairs={{0,4},{1,5},{2,6},{3,7},{4,0},{5,1},{6,2},{7,3},{8,12},{9,13},{10,... | collective-permute-start | bytes 2654216 | tf_op jit(solution)/shard_map/ppermute | solution.py:525
  (57 other events, 1203.8 us)
Sparse Core Ops, SparseCore 0:
  507.5 108.6 all-gather.2

commit v2 on v1

--- a/solution.py
+++ b/solution.py
@@ -9,13 +9,17 @@
 EPS = 1e-05
 TEMPERATURE = 0.01
 MASKED = -1000000000.0
-BOTH = ("dp", "seq")
+SEQ = ("x", "core")
+DP = ("far", "near")
+BOTH = DP + SEQ
+NEAR = ("near", "x")
+FAR = ("far",)
 EXACT = lax.Precision.HIGHEST
 BF = jnp.bfloat16
 F32 = jnp.float32
 VMEM_BYTES = 60 * 2**20
 BRIEF = pl.CostEstimate(flops=7 * 10**10, bytes_accessed=10**6, transcendentals=0)
-TICK = pl.CostEstimate(flops=1000, bytes_accessed=1000, transcendentals=0)
+TICK = pl.CostEstimate(flops=3 * 10**10, bytes_accessed=10**6, transcendentals=0)
 
 
 def dot(left, right, left_at=1, right_at=0):
@@ -136,7 +140,7 @@
     lse_out[0] = stats.T[: lse_out.shape[1]]
     ready(3)
     unit_one, inverse_one = normalize(x.astype(F32) + (dot(mixed_out[0], w_out[...]) + b_out))
-    unit_one_out[0] = unit_one
+    unit_one_out[0] = unit_one.astype(BF)
     inverse_one_out[0] = inverse_one
     hidden = unit_one * gain_one + shift_one
     hidden_low = hidden.astype(BF)
@@ -151,7 +155,7 @@
         slope_out[0, :, at] = slope.astype(BF)
         total = total + dot(low, w_down[at, :])
     unit_two, inverse_two = normalize(total)
-    unit_two_out[0] = unit_two
+    unit_two_out[0] = unit_two.astype(BF)
     inverse_two_out[0] = inverse_two
     act_held[...] = (unit_two * gain_two + shift_two).astype(BF)
     for k in range(pieces):
@@ -167,8 +171,8 @@
     units = weights[4].shape[1]
     shapes = [
         ((span, width), BF), ((span, width), BF), ((span, width), BF), ((span, width), BF),
-        ((span, width), BF), ((16, span), F32), ((span, width), F32), ((span, 1), F32),
-        ((span, width), BF), ((span, units), BF), ((span, units), BF), ((span, width), F32),
+        ((span, width), BF), ((16, span), F32), ((span, width), BF), ((span, 1), F32),
+        ((span, width), BF), ((span, units), BF), ((span, units), BF), ((span, width), BF),
         ((span, 1), F32), ((1, width), F32),
     ]
     outs = [jax.ShapeDtypeStruct((passages,) + s, t) for s, t in shapes]
@@ -213,12 +217,16 @@
     return jnp.where(live, norm_back(push, unit_two, inverse_two), 0.0)
 
 
-def hand_over(total, kept_hbm, sent_hbm, side, place, sems):
-    half = total.shape[0] // 2
+def hand_over(total, kept_hbm, sent_hbm, side, row, column, sems):
+    half, columns = total.shape[0] // 2, total.shape[1]
     own = pl.multiple_of(side * half, half)
     other = pl.multiple_of((1 - side) * half, half)
     copies = [
-        pltpu.make_async_copy(total.at[pl.ds(at, half), :], out.at[pl.ds(place, half), :], sem)
+        pltpu.make_async_copy(
+            total.at[pl.ds(at, half), :],
+            out.at[pl.ds(row, half), pl.ds(column, columns)],
+            sem,
+        )
         for at, out, sem in ((own, kept_hbm, sems.at[0]), (other, sent_hbm, sems.at[1]))
     ]
     for copy in copies:
@@ -267,7 +275,9 @@
         rows[...] = jnp.zeros_like(rows)
 
     if opening:
-        grad_hidden = second_norm_back(lens[step], push[0], unit_two[0], inverse_two[0])
+        grad_hidden = second_norm_back(
+            lens[step], push[0], unit_two[0].astype(F32), inverse_two[0]
+        )
         grad_low = grad_hidden.astype(BF)
         low_out[0] = grad_low
         rows[3:4, :] += jnp.sum(grad_low.astype(F32), axis=0, keepdims=True)
@@ -280,7 +290,7 @@
     total[total.shape[0] - width :, :] += dot(hidden_low[0], up_low, 0, 0)
     grad_hidden = grad_hidden + dot(up_low, w_up[...], 1, 1)
     if closing:
-        unit = unit_one[0]
+        unit = unit_one[0].astype(F32)
         rows[0:1, :] += jnp.sum(grad_hidden * unit, axis=0, keepdims=True)
         rows[1:2, :] += jnp.sum(grad_hidden, axis=0, keepdims=True)
         grad_one = norm_back(grad_hidden * gain_one[...], unit, inverse_one[0])
@@ -294,7 +304,7 @@
 
     @pl.when(step == last)
     def _():
-        hand_over(total, kept_hbm, sent_hbm, core[0], place, sems)
+        hand_over(total, kept_hbm, sent_hbm, core[0], place, 0, sems)
 
 
 def feed_back(lens, core, row_operands, gelu, slope, hidden_low, w_down, w_up, w_out, part, parts,
@@ -440,7 +450,7 @@
     @pl.when(step == last)
     def _():
         if closing:
-            hand_over(total, *totals_out, core[0], 0, sems)
+            hand_over(total, *totals_out, core[0], 0, 0, sems)
         else:
             after = pltpu.make_async_copy(total, totals_out[0], sems.at[1])
             after.start()
@@ -508,7 +518,7 @@
     )(lens, src, core, *operands)
 
 
-def tick(values):
+def tick(values, cost):
     operands, specs, outs, out_specs = [], [], [], []
     pairs = alias(operands, specs, outs, out_specs, values, 0)
     return pl.pallas_call(
@@ -517,7 +527,7 @@
         in_specs=specs,
         out_specs=out_specs,
         input_output_aliases=pairs,
-        cost_estimate=TICK,
+        cost_estimate=cost,
     )(*operands)
 
 
@@ -525,68 +535,114 @@
     return lax.ppermute(value, axes, [(i, i ^ amount) for i in range(devices)])
 
 
+def exchange(blocks, axes):
+    return lax.all_to_all(blocks, axes, split_axis=0, concat_axis=0, tiled=True)
+
+
 class Summing:
-    def __init__(self, kept, sent, bits, short, me, devices, plan=(), extra=None):
-        self.kept, self.sent, self.bits, self.short = kept, sent, list(bits), short
-        self.me, self.devices, self.plan, self.extra = me, devices, list(plan), extra
+    def __init__(self, kept, sent, extra=None, narrow=(NEAR,), hops=False):
+        self.kept, self.sent, self.extra = kept, sent, extra
+        self.narrow, self.hops = narrow, hops
+        self.stages = [None, NEAR, FAR]
         self.left = 0
         self.done = False
+        self.apart = None
 
     def launch(self):
-        bit = self.bits.pop(0)
-        self.narrow = bit in self.short
-        sent = self.sent.astype(BF) if self.narrow else self.sent
-        if self.extra is not None:
-            if self.narrow:
+        self.axes = self.stages.pop(0)
+        self.left = 1
+        if self.axes is None:
+            self.came = flip(self.sent, 1, BOTH, lax.axis_size(BOTH))
+            if self.extra is not None:
+                self.apart = flip(self.extra, 1, BOTH, lax.axis_size(BOTH))
+            return
+        n = lax.axis_size(self.axes)
+        rows, width = self.kept.shape
+        sent = self.value.reshape(n, rows, width)
+        if self.axes is FAR and self.hops:
+            at = lax.axis_index(FAR)
+            self.came = [
+                flip(lax.dynamic_index_in_dim(sent, at ^ k, 0, False), k, FAR, n)
+                for k in range(1, n)
+            ]
+            self.left = 2
+            return
+        spread = lambda v: jnp.broadcast_to(v[None], (n,) + v.shape)
+        more = []
+        if self.axes in self.narrow:
+            sent = sent.astype(BF)
+            if self.extra is not None:
                 high = lax.reduce_precision(self.extra, 8, 7)
                 low = lax.reduce_precision(self.extra - high, 8, 7)
                 self.extra = high + low
-                sent = jnp.concatenate([sent, high.astype(BF), low.astype(BF)], axis=0)
-            else:
-                sent = jnp.concatenate([sent, self.extra], axis=0)
-        self.came = flip(sent, 1 << bit, BOTH, self.devices)
-        self.left = self.plan.pop(0) if self.plan else 1
+                more = [spread(high.astype(BF)), spread(low.astype(BF))]
+        elif self.extra is not None:
+            more = [spread(self.extra)]
+        self.came = exchange(jnp.concatenate([sent] + more, axis=1) if more else sent, self.axes)
 
     def land(self):
+        rows = self.kept.shape[0]
+        if isinstance(self.came, list):
+            self.kept = sum(self.came, self.kept).astype(BF)
+            self.left, self.done = 0, True
+            return
+        came = self.came.astype(F32)
+        if self.axes is None:
+            value = self.kept + came
+            if self.extra is not None:
+                self.extra = self.extra + self.apart
+        else:
+            other = jnp.arange(came.shape[0]) != lax.axis_index(self.axes)
+            value = self.kept + jnp.sum(
+                jnp.where(other[:, None, None], came[:, :rows], 0.0), axis=0
+            )
+            if self.extra is not None:
+                more = jnp.sum(came[:, rows:], axis=0)
+                self.extra = jnp.sum(more.reshape((-1,) + self.extra.shape), axis=0)
         self.left = 0
-        rows = self.kept.shape[0]
-        came = self.came.astype(F32)
-        if self.extra is not None:
-            n = self.extra.shape[0]
-            more = came[rows : rows + n]
-            if self.narrow:
-                more = more + came[rows + n :]
-            self.extra = self.extra + more
-            came = came[:rows]
-        value = self.kept + came
-        if not self.bits:
+        if not self.stages:
             self.kept = value.astype(BF)
             self.done = True
             return
-        side = (self.me >> self.bits[0]) & 1
-        self.sent = lax.dynamic_slice_in_dim(value, (1 - side) * (rows // 2), rows // 2)
-        self.kept = lax.dynamic_slice_in_dim(value, side * (rows // 2), rows // 2)
+        self.value = value
+        part = value.shape[0] // lax.axis_size(self.stages[0])
+        self.kept = lax.dynamic_slice_in_dim(
+            value, lax.axis_index(self.stages[0]) * part, part
+        )
 
 
 class Gathering:
-    def __init__(self, value, bits, me, devices):
-        self.kept, self.bits, self.me, self.devices = value, list(bits)[::-1], me, devices
+    def __init__(self, value):
+        self.kept = value
+        self.stages = [FAR, NEAR, None]
         self.left = 0
-        self.done = not self.bits
+        self.done = False
 
     def launch(self):
-        self.bit = self.bits.pop(0)
-        self.came = flip(self.kept, 1 << self.bit, BOTH, self.devices)
+        self.axes = self.stages.pop(0)
         self.left = 1
+        if self.axes is None:
+            self.came = flip(self.kept, 1, BOTH, lax.axis_size(BOTH))
+        else:
+            n = lax.axis_size(self.axes)
+            self.came = exchange(
+                jnp.broadcast_to(self.kept[None], (n,) + self.kept.shape), self.axes
+            )
 
     def land(self):
-        self.kept = jnp.where(
-            ((self.me >> self.bit) & 1) == 0,
-            jnp.concatenate([self.kept, self.came], axis=0),
-            jnp.concatenate([self.came, self.kept], axis=0),
-        )
+        if self.axes is None:
+            self.kept = jnp.where(
+                lax.axis_index("core") == 0,
+                jnp.concatenate([self.kept, self.came], axis=0),
+                jnp.concatenate([self.came, self.kept], axis=0),
+            )
+        else:
+            own = jnp.arange(self.came.shape[0]) == lax.axis_index(self.axes)
+            self.kept = jnp.where(own[:, None, None], self.kept[None], self.came).reshape(
+                -1, self.kept.shape[1]
+            )
         self.left = 0
-        self.done = not self.bits
+        self.done = not self.stages
 
 
 class Homing:
@@ -609,7 +665,7 @@
 
     def launch(self):
         take = max(1, (self.n - 1) // 3)
-        self.came = [(k, flip(p, k, "seq", self.n)) for k, p in self.waiting[:take]]
+        self.came = [(k, flip(p, k, SEQ, self.n)) for k, p in self.waiting[:take]]
         self.waiting = self.waiting[take:]
         self.left = self.stretch
 
@@ -624,12 +680,11 @@
         return self.kept.reshape(n * mine, block, width)
 
 
-def in_order(every, bits):
-    n = len(bits)
-    width = every.shape[-1]
-    every = every.reshape((2,) * n + (-1, width))
-    every = every.transpose(tuple(n - 1 - b for b in bits) + (n, n + 1))
-    return every.reshape(-1, width)
+def in_order(every):
+    n_far, n_near, n_x, n_core = (lax.axis_size(axis) for axis in BOTH)
+    width = every.shape[1]
+    every = every.reshape(n_far, n_near, n_x, n_core, -1, width)
+    return every.transpose(3, 1, 2, 0, 4, 5).reshape(-1, width)
 
 
 def local(
@@ -637,9 +692,9 @@
     b_out, gain_one, shift_one, w_up, b_up, w_down, second_feedforward_offset, gain_two, shift_two,
 ):
     documents, block, width = tokens.shape
-    n_seq, n_dp = lax.axis_size("seq"), lax.axis_size("dp")
+    n_seq, n_dp = lax.axis_size(SEQ), lax.axis_size(DP)
     devices = n_seq * n_dp
-    seq_at, dp_at = lax.axis_index("seq"), lax.axis_index("dp")
+    seq_at, dp_at = lax.axis_index(SEQ), lax.axis_index(DP)
     me = dp_at * n_seq + seq_at
     mine = documents // n_seq
     batch = documents * n_dp
@@ -654,7 +709,7 @@
         pieces = []
         for k in range(n_seq):
             rows = lax.dynamic_slice_in_dim(tokens, (seq_at ^ k) * mine + first + late, count)
-            pieces.append(rows if k == 0 else flip(rows, k, "seq", n_seq))
+            pieces.append(rows if k == 0 else flip(rows, k, SEQ, n_seq))
         return pieces
 
     weights = (w_query, w_key, w_value, w_out, w_up, w_down)
@@ -666,7 +721,7 @@
     first = 0
     pieces = None
     dp_hops = n_dp.bit_length() - 1
-    hop = lambda value, bit: flip(value, 1 << bit, "dp", n_dp)
+    hop = lambda value, bit: flip(value, 1 << bit, DP, n_dp)
     spread = queries[None]
     done = min(1, dp_hops)
     if done:
@@ -724,20 +779,13 @@
     grad_gain_two = jnp.sum(each * unit_sums[:, 0, :], axis=0)
     grad_shift_two = jnp.sum(grad_pooled, axis=0)
 
-    seq_bits = n_seq.bit_length() - 1
-    top_bit = devices.bit_length() - 1
-    far_bits = tuple(range(seq_bits + 1, top_bit))
-    bits = (0, seq_bits) + tuple(range(1, seq_bits)) + far_bits
-    bits_b = tuple(range(top_bit))
-    short = range(1, seq_bits + 1)
     core = (me & 1)[None]
     feed_parts = units // width
-    heads_parts = 1
     feed = (gelu, slope, hidden_low, w_down, w_up, w_out)
     flying = []
 
-    def begin(kept, sent, bits, *plan, extra=None):
-        one = Summing(kept, sent, bits, short, me, devices, plan, extra)
+    def begin(kept, sent, *more):
+        one = Summing(kept, sent, *more)
         flying.append(one)
         return one
 
@@ -750,16 +798,15 @@
     def landing(kept):
         for one, value in zip(list(flying), kept):
             one.kept = value
-            if one.done:
-                flying.remove(one)
-                continue
             one.left -= 1
             if not one.left:
                 one.land()
-
+            if one.done:
+                flying.remove(one)
+
+    chunks = [None]
     up_biases = []
     operands = (push, unit_two, inverse_two)
-    chunks = []
     for part in range(feed_parts):
         closing = part == feed_parts - 1
         second = part % 2
@@ -784,52 +831,50 @@
             rows_a, grad_low = rows, low
         operands = (grad_low, grad_hidden)
         if second:
-            chunks.append(begin(kept, sent, *((bits_b, 1, 2) if closing else (bits,))))
+            chunks.append(begin(kept, sent, None, (NEAR,), closing))
+            if chunks[0] is None:
+                chunks.pop(0)
     grad_one, grad_mixed, rows_b = grad_hidden, low, rows
-    biases = []
-    grad_in = grad_one
-    for part in range(heads_parts):
+    total, homes = None, ()
+    bias = 0.0
+    for first, count in ((0, mine - mine // 2), (mine - mine // 2, mine // 2)):
+        closing = first > 0
         riders = riding()
         outs = attention_back(
-            lens, src, core, n_seq, x, q, k, v, lse, grad_mixed, grad_in,
-            (w_query, w_key, w_value), part, heads_parts, 0, mine, 0, None, True, (), riders,
+            lens, src, core, n_seq, x, q, k, v, lse, grad_mixed, grad_one,
+            (w_query, w_key, w_value), 0, 1, first, count, first, total, closing, homes, riders,
         )
-        n = n_seq if part == heads_parts - 1 else 1
-        landing(outs[n + 3 :])
-        grad_in = outs[0]
-        biases.append(outs[n])
-        kept, sent = outs[n + 1 : n + 3]
-        extra = None
-        if part == heads_parts - 1:
-            extra = jnp.concatenate(
-                [
-                    jnp.concatenate(biases, axis=1), rows_b[0:3], rows_a[3:4],
-                    row(grad_gain_two), row(grad_shift_two),
-                    jnp.concatenate(up_biases, axis=1).reshape(feed_parts, width),
-                    jnp.zeros((-(8 + feed_parts) % 16, width), F32),
-                ],
-                axis=0,
-            )
-        extra = jnp.concatenate([extra, jnp.zeros((-len(extra) % 3, width), F32)], axis=0)
-        chunks.append(begin(kept, sent, bits, extra=extra.reshape(-1, 3 * width)))
-    homes = Homing(outs[:n_seq], F32, seq_at, 2)
-    flying.append(homes)
-    first, second, heads = chunks
-    feed = attention = None
-    while flying:
-        if first.done and second.done and feed is None:
-            feed = jnp.concatenate([first.kept, second.kept], axis=0)
-            feed = lax.all_gather(feed, BOTH, axis=0)
+        landing(outs[n_seq + (3 if closing else 2) :])
+        homes, bias, total = outs[:n_seq], bias + outs[n_seq], outs[n_seq + 1]
+    kept, sent = outs[n_seq + 1 : n_seq + 3]
+    extra = jnp.concatenate(
+        [
+            bias, rows_b[0:3], rows_a[3:4], row(grad_gain_two), row(grad_shift_two),
+            jnp.concatenate(up_biases, axis=1).reshape(feed_parts, width),
+            jnp.zeros((-(8 + feed_parts) % 3, width), F32),
+        ],
+        axis=0,
+    )
+    heads = begin(kept, sent, extra.reshape(-1, 3 * width), (NEAR, FAR))
+    homes = Homing(homes, F32, seq_at, 1)
+    all_a, all_b = chunks
+    attention = gathered = None
+    every = lambda one: lax.all_gather(one.kept, BOTH, axis=0, tiled=True)
+    gathered_a = every(all_a)
+    steps = 0
+    while flying or steps <= 2:
+        if steps == 2:
+            flying.append(homes)
+        if all_b.done and gathered is None:
+            gathered = every(all_b)
         if heads.done and attention is None:
-            attention = Gathering(heads.kept, bits, me, devices)
+            attention = Gathering(heads.kept)
             flying.append(attention)
-        flying = [one for one in flying if not one.done]
-        if flying:
-            landing(tick(riding()))
+        landing(tick(riding(), TICK if steps else BRIEF))
+        steps += 1
     small = heads.extra.reshape(-1, width)
     attention = attention.kept
-    cut = first.kept.shape[0]
-    all_a, all_b = in_order(feed[:, :cut], bits), in_order(feed[:, cut:], bits_b)
+    all_a, all_b = in_order(gathered_a), in_order(gathered)
     activations, grad_tokens = activations.whole(), homes.whole()
     grads = [attention[:, n * width : (n + 1) * width].astype(F32) for n in range(3)]
     two = 2 * width
@@ -867,6 +912,8 @@
 
 
 def solution(mesh):
-    in_specs = (P("dp", "seq", None), P(), P("dp"), P(), P("dp", None)) + (P(),) * 15
-    out_specs = (P(), P("dp", "seq", None), P("dp", "seq", None)) + (P(),) * 15
-    return jax.shard_map(local, mesh=mesh, in_specs=in_specs, out_specs=out_specs, check_vma=False)
+    dp, seq = mesh.shape["dp"], mesh.shape["seq"]
+    finer = jax.sharding.Mesh(mesh.devices.reshape(dp // 2, 2, seq // 2, 2), BOTH)
+    in_specs = (P(DP, SEQ, None), P(), P(DP), P(), P(DP, None)) + (P(),) * 15
+    out_specs = (P(), P(DP, SEQ, None), P(DP, SEQ, None)) + (P(),) * 15
+    return jax.shard_map(local, mesh=finer, in_specs=in_specs, out_specs=out_specs, check_vma=False)

time: 659 us -> 551 us (0.84)
  waiting for transfers between devices: 205 us -> 102 us
  starting transfers between devices: 38.1 us -> 51.9 us
  local copies, waits for them, and re-layouts: 64.6 us -> 53.6 us
    ppermute x40 -> x28, waiting for transfers between devices: 205 us -> 34.2 us  [flip(): return lax.ppermute(value, axes, [(i, i ^ amount) for i in range(devices)])]
    all_to_all x0 -> x7, waiting for transfers between devices: none -> 67.3 us  [exchange(): return lax.all_to_all(blocks, axes, split_axis=0, concat_axis=0, tiled=True)]
    all_to_all x0 -> x7, starting transfers between devices: none -> 27.2 us  [exchange(): return lax.all_to_all(blocks, axes, split_axis=0, concat_axis=0, tiled=True)]
    convert_element_type x3 -> x7, other arithmetic: 2.44 us -> 23.7 us  [the longest x4 21.7 us: launch(): sent = sent.astype(BF)]
    add x15 -> x3, other arithmetic: 23 us -> 2.11 us  [the longest x2 1.41 us: land(): self.kept + jnp.sum(jnp.where(other[:, None, None], came[:, :rows], 0.0),...]
    ppermute x40 -> x28, starting transfers between devices: 38.1 us -> 24.7 us  [flip(): return lax.ppermute(value, axes, [(i, i ^ amount) for i in range(devices)])]
    pallas_call x2, Pallas kernels: 100 us -> 87.4 us  [forward(): pl.pallas_call(kernel, out_shape=outs, grid_spec=pltpu.PrefetchScalarGrid...]
    pallas_call x1 -> x2, Pallas kernels: 62.4 us -> 72.8 us  [attention_back(): pl.pallas_call(kernel, out_shape=outs, grid_spec=pltpu.PrefetchScalarGrid...]
  transfers between devices with their start and end apart: 41 -> 37, of which waited for: 17 -> 14; matrix products, arithmetic and copies ran while one was open for 16% -> 17% of each run, Pallas kernels for 24% -> 30%
where the time goes in v2:
time: 551 us; the launch traced here: 540 us
  Pallas kernels  246 us (45%)
  waiting for transfers between devices  102 us (19%)
  other arithmetic  67.7 us (12%)
  local copies, waits for them, and re-layouts  53.6 us (10%)
  starting transfers between devices  51.9 us (9%)
  between operations  18.3 us (3%)
    pallas_call x2, Pallas kernels, forward(): pl.pallas_call(kernel, out_shape=outs, grid_spec=pltpu.PrefetchScalarGrid...  87.4 us
    pallas_call x4, Pallas kernels, feed_back(): pl.pallas_call(kernel, out_shape=outs, grid_spec=pltpu.PrefetchScalarGrid...  85.6 us
    pallas_call x2, Pallas kernels, attention_back(): pl.pallas_call(kernel, out_shape=outs, grid_spec=pltpu.PrefetchScalarGrid...  72.8 us
    all_to_all x7, waiting for transfers between devices, exchange(): return lax.all_to_all(blocks, axes, split_axis=0, concat_axis=0, tiled=True)  67.3 us
    ppermute x28, waiting for transfers between devices, flip(): return lax.ppermute(value, axes, [(i, i ^ amount) for i in range(devices)])  34.2 us
    all_to_all x7, starting transfers between devices, exchange(): return lax.all_to_all(blocks, axes, split_axis=0, concat_axis=0, tiled=True)  27.2 us
    ppermute x28, starting transfers between devices, flip(): return lax.ppermute(value, axes, [(i, i ^ amount) for i in range(devices)])  24.7 us
    convert_element_type x4, other arithmetic, launch(): sent = sent.astype(BF)  21.7 us
  transfers between devices with their start and end apart: 37, of which 14 were waited for; matrix products, arithmetic and copies ran while one was open for 17% of the time, Pallas kernels for 30%

profile of v2, /device:TPU:0, one launch (start us, length us, event | category | flops | bytes accessed | tf_op | source)
XLA Modules:
  0.0 539.9 jit_solution(10470017169667357176)
XLA Ops:
  32.6 25.0 %shard_map.331 = (bf16[4,512,768]{2,1,0:T(8,128)(2,1)}, bf16[4,512,768]{2,1,0:T(8,128)(2,1)}, bf16[4,512,768]{2,1,0:T(8,128)(2,1)}, bf16[4,512,768]{2,1,0:T(8,12...) custom-call(s32[4]{0:T(128)} %get-tuple-element.232.refs_0_, ...), custom_call_target="tpu_custom_call", output_to_operand_aliasing={{18}: (13, {})} | custom-call | flops 70000001024 | bytes 1000000 | tf_op jit(solution)/shard_map/pallas_call | solution.py:198
  61.6 4.8 collective-permute-done.8
  67.6 62.4 %shard_map.332 = (bf16[4,512,768]{2,1,0:T(8,128)(2,1)}, bf16[4,512,768]{2,1,0:T(8,128)(2,1)}, bf16[4,512,768]{2,1,0:T(8,128)(2,1)}, bf16[4,512,768]{2,1,0:T(8,12...) custom-call(s32[4]{0:T(128)} %get-tuple-element.232.refs_0_, ...), custom_call_target="tpu_custom_call", output_to_operand_aliasing={{0}: (13, {}), {1}: (14, {}), {2}: (15, {}), {3}: (16, {}),... | custom-call | flops 70000001024 | bytes 1000000 | tf_op jit(solution)/shard_map/pallas_call | solution.py:198
  152.7 19.4 %shard_map.333 = (f32[4,512,768]{2,1,0:T(8,128)}, bf16[4,512,768]{2,1,0:T(8,128)(2,1)}, f32[1,768]{1,0:T(1,128)}, f32[8,768]{1,0:T(8,128)}, f32[1536,768]{1,0:T(...) custom-call(s32[4]{0:T(128)} %get-tuple-element.232.refs_0_, ...), custom_call_target="tpu_custom_call", output_to_operand_aliasing={{6}: (10, {}), {7}: (11, {}), {8}: (12, {}), {9}: (13, {})} | custom-call | flops 70000001024 | bytes 1000000 | tf_op jit(solution)/shard_map/pallas_call | solution.py:352
  174.9 19.2 %shard_map.334 = (f32[4,512,768]{2,1,0:T(8,128)}, bf16[4,512,768]{2,1,0:T(8,128)(2,1)}, f32[1,768]{1,0:T(1,128)}, f32[8,768]{1,0:T(8,128)}, f32[1536,768]{1,0:T(...) custom-call(s32[4]{0:T(128)} %get-tuple-element.232.refs_0_, ...), custom_call_target="tpu_custom_call", output_to_operand_aliasing={{4}: (9, {}), {5}: (10, {}), {6}: (11, {})} | custom-call | flops 70000001024 | bytes 1000000 | tf_op jit(solution)/shard_map/pallas_call | solution.py:352
  199.5 19.2 %shard_map.335 = (f32[4,512,768]{2,1,0:T(8,128)}, bf16[4,512,768]{2,1,0:T(8,128)(2,1)}, f32[1,768]{1,0:T(1,128)}, f32[8,768]{1,0:T(8,128)}, f32[1920,768]{1,0:T(...) custom-call(s32[4]{0:T(128)} %get-tuple-element.232.refs_0_, ...), custom_call_target="tpu_custom_call", output_to_operand_aliasing={{6}: (9, {}), {7}: (10, {})} | custom-call | flops 70000001024 | bytes 1000000 | tf_op jit(solution)/shard_map/pallas_call | solution.py:352
  219.6 7.4 %fusion.38 = (bf16[1536,768]{1,0:T(8,128)(2,1)}, f32[1536,768]{1,0:T(8,128)}) fusion(f32[1536,768]{1,0:T(8,128)} %get-tuple-element.158, f32[1536,768]{1,0:T(8,128)} %collective-permute-done.16), kind=kLoop, calls=%fused_computation.161 | loop fusion | flops 2359296 | bytes 16515072 | tf_op jit(solution)/shard_map/convert_element_type | solution.py:573
  233.1 27.9 %shard_map.336 = (f32[4,512,768]{2,1,0:T(8,128)}, bf16[4,512,768]{2,1,0:T(8,128)(2,1)}, f32[1,768]{1,0:T(1,128)}, f32[8,768]{1,0:T(8,128)}, f32[1920,768]{1,0:T(...) custom-call(s32[4]{0:T(128)} %get-tuple-element.232.refs_0_, ...), custom_call_target="tpu_custom_call", output_to_operand_aliasing={{4}: (14, {}), {5}: (15, {}), {6}: (16, {}), {7}: (17, {})} | custom-call | flops 70000001024 | bytes 1000000 | tf_op jit(solution)/shard_map/pallas_call | solution.py:352
  267.6 3.8 all-to-all-start.6
  271.4 36.3 %shard_map.337 = (bf16[4,128,768]{2,1,0:T(8,128)(2,1)}, bf16[4,128,768]{2,1,0:T(8,128)(2,1)}, bf16[4,128,768]{2,1,0:T(8,128)(2,1)}, bf16[4,128,768]{2,1,0:T(8,12...) custom-call(s32[4]{0:T(128)} %get-tuple-element.232.refs_0_, ...), custom_call_target="tpu_custom_call", output_to_operand_aliasing={{6}: (13, {}), {7}: (14, {})} | custom-call | flops 70000001024 | bytes 1000000 | tf_op jit(solution)/shard_map/pallas_call | solution.py:503
  309.5 8.8 %fusion.37 = (bf16[1920,768]{1,0:T(8,128)(2,1)}, f32[1920,768]{1,0:T(8,128)}) fusion(f32[1920,768]{1,0:T(8,128)} %get-tuple-element.176, f32[1920,768]{1,0:T(8,128)} %collective-permute-done.18), kind=kLoop, calls=%fused_computation.160 | loop fusion | flops 2949120 | bytes 20643840 | tf_op jit(solution)/shard_map/convert_element_type | solution.py:573
  318.3 4.0 all-to-all-start.1
  324.9 36.5 %shard_map.338 = (bf16[4,128,768]{2,1,0:T(8,128)(2,1)}, bf16[4,128,768]{2,1,0:T(8,128)(2,1)}, bf16[4,128,768]{2,1,0:T(8,128)(2,1)}, bf16[4,128,768]{2,1,0:T(8,12...) custom-call(s32[4]{0:T(128)} %get-tuple-element.232.refs_0_, ...), custom_call_target="tpu_custom_call", output_to_operand_aliasing={{0}: (14, {}), {1}: (15, {}), {2}: (16, {}), {3}: (17, {}),... | custom-call | flops 70000001024 | bytes 1000000 | tf_op jit(solution)/shard_map/pallas_call | solution.py:503
  375.9 5.4 %fusion.36 = (bf16[384,2304]{1,0:T(8,128)(2,1)S(1)}, f32[384,2304]{1,0:T(8,128)}) fusion(f32[384,2304]{1,0:T(8,128)} %get-tuple-element.181, f32[384,2304]{1,0:T(8,128)} %collective-permute-done.19), kind=kLoop, calls=%fused_computation.159 | loop fusion | flops 1769472 | bytes 12386304 | tf_op jit(solution)/shard_map/convert_element_type | solution.py:573
  388.5 5.5 %collective-permute-done.25 = f32[120,768]{1,0:T(8,128)S(1)} collective-permute-done((f32[120,768]{1,0:T(8,128)S(1)}, f32[120,768]{1,0:T(8,128)S(1)}, u32[]{:S(2)}, u32[]{:S(2)}) %collective-permute-start.25) | collective-permute-done | bytes 368672 | tf_op jit(solution)/shard_map/ppermute | solution.py:535
  394.0 10.3 %collective-permute-done.26 = f32[120,768]{1,0:T(8,128)} collective-permute-done((f32[120,768]{1,0:T(8,128)S(1)}, f32[120,768]{1,0:T(8,128)}, u32[]{:S(2)}, u32[]{:S(2)}) %collective-permute-start.26) | collective-permute-done | bytes 368672 | tf_op jit(solution)/shard_map/ppermute | solution.py:535
  406.3 4.3 all-to-all-done.2
  413.1 5.1 all-to-all-start.3
  421.4 16.6 %all-to-all-done.3 = bf16[4,32,2304]{2,1,0:T(8,128)(2,1)S(1)} async-done(((bf16[4,32,2304]{2,1,0:T(8,128)(2,1)}), bf16[4,32,2304]{2,1,0:T(8,128)(2,1)S(1)}, u32[]{:S(2)}, u32[]{:S(2)}) %all-to-all-start.3) | async-done | bytes 589856 | tf_op jit(solution)/shard_map/all_to_all | solution.py:539
  445.1 16.9 %all-to-all-done.4 = bf16[4,24,2304]{2,1,0:T(8,128)(2,1)S(1)} async-done(((bf16[4,24,2304]{2,1,0:T(8,128)(2,1)}), bf16[4,24,2304]{2,1,0:T(8,128)(2,1)S(1)}, u32[]{:S(2)}, u32[]{:S(2)}) %all-to-all-start.4) | async-done | bytes 442400 | tf_op jit(solution)/shard_map/all_to_all | solution.py:539
  468.0 29.4 %all-to-all-done.5 = bf16[4,96,2304]{2,1,0:T(8,128)(2,1)S(1)} async-done(((bf16[4,96,2304]{2,1,0:T(8,128)(2,1)}), bf16[4,96,2304]{2,1,0:T(8,128)(2,1)S(1)}, u32[]{:S(2)}, u32[]{:S(2)}) %all-to-all-start.5) | async-done | bytes 1769504 | tf_op jit(solution)/shard_map/all_to_all | solution.py:539
  510.7 3.8 maximum_select_fusion
  521.3 4.5 maximum_convert_fusion.1
  527.4 4.3 maximum_convert_fusion
  (275 shorter events, 140.9 us)
Async XLA Ops:
  11.6 21.0 %collective-permute-start.4 = (bf16[1,128,768]{2,1,0:T(8,128)(2,1)S(1)}, bf16[1,128,768]{2,1,0:T(8,128)(2,1)}, u32[]{:S(2)}, u32[]{:S(2)}) collective-permute-start(bf16[1,128,768]{2,1,0:T(8,128)(2,1)S(1)} %get-tuple-element.245), channel_id=1, source_target_pairs={{0,1},{1,0},{2,3},{3,2},{4,5},{5,4},{6,7},{7,6},{8,9},{9,8},{10,11... | collective-permute-start | bytes 589832 | tf_op jit(solution)/shard_map/ppermute | solution.py:535
  12.2 20.4 %collective-permute-start.5 = (bf16[1,128,768]{2,1,0:T(8,128)(2,1)S(1)}, bf16[1,128,768]{2,1,0:T(8,128)(2,1)}, u32[]{:S(2)}, u32[]{:S(2)}) collective-permute-start(bf16[1,128,768]{2,1,0:T(8,128)(2,1)S(1)} %get-tuple-element.242), channel_id=1, source_target_pairs={{0,2},{1,3},{2,0},{3,1},{4,6},{5,7},{6,4},{7,5},{8,10},{9,11},{10,... | collective-permute-start | bytes 589832 | tf_op jit(solution)/shard_map/ppermute | solution.py:535
  30.7 35.6 %collective-permute-start.1 = (bf16[3,128,768]{2,1,0:T(8,128)(2,1)S(1)}, bf16[3,128,768]{2,1,0:T(8,128)(2,1)S(1)}, u32[]{:S(2)}, u32[]{:S(2)}) collective-permute-start(bf16[3,128,768]{2,1,0:T(8,128)(2,1)S(1)} %get-tuple-element.248), channel_id=1, source_target_pairs={{0,1},{1,0},{2,3},{3,2},{4,5},{5,4},{6,7},{7,6},{8,9},{9,8},{10,11... | collective-permute-start | bytes 1769480 | tf_op jit(solution)/shard_map/ppermute | solution.py:535
  30.7 35.6 %collective-permute-start.2 = (bf16[3,128,768]{2,1,0:T(8,128)(2,1)S(1)}, bf16[3,128,768]{2,1,0:T(8,128)(2,1)S(1)}, u32[]{:S(2)}, u32[]{:S(2)}) collective-permute-start(bf16[3,128,768]{2,1,0:T(8,128)(2,1)S(1)} %get-tuple-element.247), channel_id=1, source_target_pairs={{0,2},{1,3},{2,0},{3,1},{4,6},{5,7},{6,4},{7,5},{8,10},{9,11},{10,... | collective-permute-start | bytes 1769480 | tf_op jit(solution)/shard_map/ppermute | solution.py:535
  32.2 34.1 %collective-permute-start.3 = (bf16[3,128,768]{2,1,0:T(8,128)(2,1)S(1)}, bf16[3,128,768]{2,1,0:T(8,128)(2,1)S(1)}, u32[]{:S(2)}, u32[]{:S(2)}) collective-permute-start(bf16[3,128,768]{2,1,0:T(8,128)(2,1)S(1)} %get-tuple-element.246), channel_id=1, source_target_pairs={{0,3},{1,2},{2,1},{3,0},{4,7},{5,6},{6,5},{7,4},{8,11},{9,10},{10,... | collective-permute-start | bytes 1769480 | tf_op jit(solution)/shard_map/ppermute | solution.py:535
  172.0 26.5 %collective-permute-start.14 = (bf16[4,128,768]{2,1,0:T(8,128)(2,1)}, bf16[4,128,768]{2,1,0:T(8,128)(2,1)S(1)}, u32[]{:S(2)}, u32[]{:S(2)}) collective-permute-start(bf16[4,128,768]{2,1,0:T(8,128)(2,1)} %get-tuple-element.148), channel_id=1, source_target_pairs={{0,1},{1,0},{2,3},{3,2},{4,5},{5,4},{6,7},{7,6},{8,9},{9,8},{10,11... | collective-permute-start | bytes 2359304 | tf_op jit(solution)/shard_map/ppermute | solution.py:535
  194.1 25.5 %collective-permute-start.16 = (f32[1536,768]{1,0:T(8,128)}, f32[1536,768]{1,0:T(8,128)}, u32[]{:S(2)}, u32[]{:S(2)}) collective-permute-start(f32[1536,768]{1,0:T(8,128)} %get-tuple-element.159), channel_id=1, source_target_pairs={{0,1},{1,0},{2,3},{3,2},{4,5},{5,4},{6,7},{7,6},{8,9},{9,8},{10,11... | collective-permute-start | bytes 14155784 | tf_op jit(solution)/shard_map/ppermute | solution.py:535
  194.2 24.5 %collective-permute-start.15 = (bf16[4,128,768]{2,1,0:T(8,128)(2,1)}, bf16[4,128,768]{2,1,0:T(8,128)(2,1)S(1)}, u32[]{:S(2)}, u32[]{:S(2)}) collective-permute-start(bf16[4,128,768]{2,1,0:T(8,128)(2,1)} %get-tuple-element.157), channel_id=1, source_target_pairs={{0,2},{1,3},{2,0},{3,1},{4,6},{5,7},{6,4},{7,5},{8,10},{9,11},{10,... | collective-permute-start | bytes 2359304 | tf_op jit(solution)/shard_map/ppermute | solution.py:535
  198.2 302.8 %collective-permute-start.17 = (bf16[4,128,768]{2,1,0:T(8,128)(2,1)}, bf16[4,128,768]{2,1,0:T(8,128)(2,1)}, u32[]{:S(2)}, u32[]{:S(2)}) collective-permute-start(bf16[4,128,768]{2,1,0:T(8,128)(2,1)} %get-tuple-element.161), channel_id=1, source_target_pairs={{0,3},{1,2},{2,1},{3,0},{4,7},{5,6},{6,5},{7,4},{8,11},{9,10},{10,... | collective-permute-start | bytes 2359304 | tf_op jit(solution)/shard_map/ppermute | solution.py:535
  227.0 37.0 %all-to-all-start = ((bf16[4,384,768]{2,1,0:T(8,128)(2,1)}), bf16[4,384,768]{2,1,0:T(8,128)(2,1)S(1)}, u32[]{:S(2)}, u32[]{:S(2)}) async-start(bf16[4,384,768]{2,1,0:T(8,128)(2,1)} %bitcast.86), calls=%async_computation | async-start | bytes 4718592 | tf_op jit(solution)/shard_map/all_to_all | solution.py:539
  260.9 48.6 %collective-permute-start.18 = (f32[1920,768]{1,0:T(8,128)}, f32[1920,768]{1,0:T(8,128)}, u32[]{:S(2)}, u32[]{:S(2)}) collective-permute-start(f32[1920,768]{1,0:T(8,128)} %get-tuple-element.177), channel_id=1, source_target_pairs={{0,1},{1,0},{2,3},{3,2},{4,5},{5,4},{6,7},{7,6},{8,9},{9,8},{10,11... | collective-permute-start | bytes 17694728 | tf_op jit(solution)/shard_map/ppermute | solution.py:535
  267.6 40.1 %all-to-all-start.6 = ((f32[4,96,768]{2,1,0:T(8,128)}), f32[4,96,768]{2,1,0:T(8,128)S(1)}, u32[]{:S(2)}, u32[]{:S(2)}) async-start(f32[4,96,768]{2,1,0:T(8,128)} %bitcast.36), calls=%async_computation.6 | async-start | bytes 2359296 | tf_op jit(solution)/shard_map/all_to_all | solution.py:539
  271.4 234.5 %all-gather.5.cloned.1.call-start = ((), (), s32[]{:S(2)}) async-start(), calls=%async_computation.8 | async-start | bytes 4866048 | tf_op jit(solution)/shard_map/all_gather | solution.py:862
  318.3 50.6 %all-to-all-start.1 = ((bf16[4,480,768]{2,1,0:T(8,128)(2,1)}), bf16[4,480,768]{2,1,0:T(8,128)(2,1)S(1)}, u32[]{:S(2)}, u32[]{:S(2)}) async-start(bf16[4,480,768]{2,1,0:T(8,128)(2,1)} %bitcast.19), calls=%async_computation.1 | async-start | bytes 5898240 | tf_op jit(solution)/shard_map/all_to_all | solution.py:539
  362.9 56.1 %collective-permute-start.21 = (bf16[4,128,768]{2,1,0:T(8,128)(2,1)}, bf16[4,128,768]{2,1,0:T(8,128)(2,1)}, u32[]{:S(2)}, u32[]{:S(2)}) collective-permute-start(bf16[4,128,768]{2,1,0:T(8,128)(2,1)} %get-tuple-element.194), channel_id=1, source_target_pairs={{0,2},{1,3},{2,0},{3,1},{4,6},{5,7},{6,4},{7,5},{8,10},{9,11},{10,... | collective-permute-start | bytes 2359304 | tf_op jit(solution)/shard_map/ppermute | solution.py:535
  371.3 22.7 %collective-permute-start.25 = (f32[120,768]{1,0:T(8,128)S(1)}, f32[120,768]{1,0:T(8,128)S(1)}, u32[]{:S(2)}, u32[]{:S(2)}) collective-permute-start(f32[120,768]{1,0:T(8,128)S(1)} %get-tuple-element.250), channel_id=1, source_target_pairs={{0,8},{8,0},{16,24},{24,16},{1,9},{9,1},{17,25},{25,17},{2,10},{10... | collective-permute-start | bytes 1105928 | tf_op jit(solution)/shard_map/ppermute | solution.py:535
  373.4 30.9 %collective-permute-start.26 = (f32[120,768]{1,0:T(8,128)S(1)}, f32[120,768]{1,0:T(8,128)}, u32[]{:S(2)}, u32[]{:S(2)}) collective-permute-start(f32[120,768]{1,0:T(8,128)S(1)} %get-tuple-element.252), channel_id=1, source_target_pairs={{0,16},{8,24},{16,0},{24,8},{1,17},{9,25},{17,1},{25,9},{2,18},{10... | collective-permute-start | bytes 1105928 | tf_op jit(solution)/shard_map/ppermute | solution.py:535
  375.8 28.5 %collective-permute-start.27 = (f32[120,768]{1,0:T(8,128)S(1)}, f32[120,768]{1,0:T(8,128)}, u32[]{:S(2)}, u32[]{:S(2)}) collective-permute-start(f32[120,768]{1,0:T(8,128)S(1)} %get-tuple-element.251), channel_id=1, source_target_pairs={{0,24},{8,16},{16,8},{24,0},{1,25},{9,17},{17,9},{25,1},{2,26},{10... | collective-permute-start | bytes 1105928 | tf_op jit(solution)/shard_map/ppermute | solution.py:535
  382.7 27.9 %all-to-all-start.2 = ((bf16[4,104,2304]{2,1,0:T(8,128)(2,1)}), bf16[4,104,2304]{2,1,0:T(8,128)(2,1)S(1)}, u32[]{:S(2)}, u32[]{:S(2)}) async-start(bf16[4,104,2304]{2,1,0:T(8,128)(2,1)} %pad_maximum_fusion), calls=%async_computation.2 | async-start | bytes 3833856 | tf_op jit(solution)/shard_map/all_to_all | solution.py:539
  386.3 131.4 %all-gather.3.cloned.1.call-start = ((), (), s32[]{:S(2)}) async-start(), calls=%async_computation.7 | async-start | bytes 6082560 | tf_op jit(solution)/shard_map/all_gather | solution.py:862
  394.0 48.6 %collective-permute-start.22 = (bf16[4,128,768]{2,1,0:T(8,128)(2,1)}, bf16[4,128,768]{2,1,0:T(8,128)(2,1)}, u32[]{:S(2)}, u32[]{:S(2)}) collective-permute-start(bf16[4,128,768]{2,1,0:T(8,128)(2,1)} %get-tuple-element.197), channel_id=1, source_target_pairs={{0,3},{1,2},{2,1},{3,0},{4,7},{5,6},{6,5},{7,4},{8,11},{9,10},{10,... | collective-permute-start | bytes 2359304 | tf_op jit(solution)/shard_map/ppermute | solution.py:535
  413.1 24.9 %all-to-all-start.3 = ((bf16[4,32,2304]{2,1,0:T(8,128)(2,1)}), bf16[4,32,2304]{2,1,0:T(8,128)(2,1)S(1)}, u32[]{:S(2)}, u32[]{:S(2)}) async-start(bf16[4,32,2304]{2,1,0:T(8,128)(2,1)} %pad_maximum_fusion.1), calls=%async_computation.3 | async-start | bytes 1179648 | tf_op jit(solution)/shard_map/all_to_all | solution.py:539
  439.1 22.9 %all-to-all-start.4 = ((bf16[4,24,2304]{2,1,0:T(8,128)(2,1)}), bf16[4,24,2304]{2,1,0:T(8,128)(2,1)S(1)}, u32[]{:S(2)}, u32[]{:S(2)}) async-start(bf16[4,24,2304]{2,1,0:T(8,128)(2,1)} %broadcast_in_dim.281), calls=%async_computation.4 | async-start | bytes 884736 | tf_op jit(solution)/shard_map/all_to_all | solution.py:539
  464.4 33.1 %all-to-all-start.5 = ((bf16[4,96,2304]{2,1,0:T(8,128)(2,1)}), bf16[4,96,2304]{2,1,0:T(8,128)(2,1)S(1)}, u32[]{:S(2)}, u32[]{:S(2)}) async-start(bf16[4,96,2304]{2,1,0:T(8,128)(2,1)} %broadcast_in_dim.286), calls=%async_computation.5 | async-start | bytes 3538944 | tf_op jit(solution)/shard_map/all_to_all | solution.py:539
  (50 other events, 900.1 us)
Sparse Core Ops, SparseCore 0:
  309.6 81.4 all-gather.4
  406.5 100.8 all-gather.2

commit v3 on v2

--- a/solution.py
+++ b/solution.py
@@ -19,6 +19,7 @@
 F32 = jnp.float32
 VMEM_BYTES = 60 * 2**20
 BRIEF = pl.CostEstimate(flops=7 * 10**10, bytes_accessed=10**6, transcendentals=0)
+LIGHT = pl.CostEstimate(flops=1000, bytes_accessed=1000, transcendentals=0)
 TICK = pl.CostEstimate(flops=3 * 10**10, bytes_accessed=10**6, transcendentals=0)
 
 
@@ -535,6 +536,35 @@
     return lax.ppermute(value, axes, [(i, i ^ amount) for i in range(devices)])
 
 
+def land_kernel(at, kept, came, low, own):
+    value = kept[...] + came[...]
+    low[...] = value.astype(BF)
+
+    @pl.when(pl.program_id(0) == at[0])
+    def _():
+        own[...] = value
+
+
+def land_first(kept, came, at, n):
+    rows, width = kept.shape
+    part = rows // n
+    each = pl.BlockSpec((part, width), lambda i, *_: (i, 0))
+    return pl.pallas_call(
+        land_kernel,
+        out_shape=[
+            jax.ShapeDtypeStruct((rows, width), BF), jax.ShapeDtypeStruct((part, width), F32)
+        ],
+        grid_spec=pltpu.PrefetchScalarGridSpec(
+            num_scalar_prefetch=1,
+            grid=(n,),
+            in_specs=[each, each],
+            out_specs=[each, whole((part, width))],
+        ),
+        compiler_params=pltpu.CompilerParams(vmem_limit_bytes=VMEM_BYTES),
+        cost_estimate=LIGHT,
+    )(at[None], kept, came)
+
+
 def exchange(blocks, axes):
     return lax.all_to_all(blocks, axes, split_axis=0, concat_axis=0, tiled=True)
 
@@ -588,9 +618,13 @@
             return
         came = self.came.astype(F32)
         if self.axes is None:
-            value = self.kept + came
             if self.extra is not None:
                 self.extra = self.extra + self.apart
+            self.value, self.kept = land_first(
+                self.kept, came, lax.axis_index(NEAR), lax.axis_size(NEAR)
+            )
+            self.left = 0
+            return
         else:
             other = jnp.arange(came.shape[0]) != lax.axis_index(self.axes)
             value = self.kept + jnp.sum(
@@ -705,12 +739,12 @@
     def arriving(first, count, before):
         late = 0
         if before is not None:
-            late = (before[-1][0, 0, 0] != before[-1][0, 0, 0]).astype(jnp.int32)
+            late = (before[0, 0, 0] != before[0, 0, 0]).astype(jnp.int32)
         pieces = []
         for k in range(n_seq):
             rows = lax.dynamic_slice_in_dim(tokens, (seq_at ^ k) * mine + first + late, count)
             pieces.append(rows if k == 0 else flip(rows, k, SEQ, n_seq))
-        return pieces
+        return pieces, rows
 
     weights = (w_query, w_key, w_value, w_out, w_up, w_down)
     row = lambda v: v[None, :]
@@ -719,7 +753,7 @@
     vectors = jnp.concatenate(vectors).reshape(-1, width)
     saved = None
     first = 0
-    pieces = None
+    sent = None
     dp_hops = n_dp.bit_length() - 1
     hop = lambda value, bit: flip(value, 1 << bit, DP, n_dp)
     spread = queries[None]
@@ -727,7 +761,7 @@
     if done:
         spread = jnp.concatenate([spread, hop(spread, 0)], axis=0)
     for count in (1, mine - 1):
-        pieces = arriving(first, count, pieces)
+        pieces, sent = arriving(first, count, sent)
         came = [hop(spread, done)] if done < dp_hops else []
         *saved, spread = forward(
             lens, src, pieces, weights, vectors, mine, first, saved, (spread,)

time: 551 us -> 550 us (level)
  Pallas kernels: 246 us -> 275 us
  other arithmetic: 67.7 us -> 45.8 us
  local copies, waits for them, and re-layouts: 53.6 us -> 41.3 us
    convert_element_type x4 -> x1, other arithmetic: 21.7 us -> 0.1 us  [launch(): sent = sent.astype(BF)]
    pallas_call x0 -> x3, Pallas kernels: none -> 18.1 us  [land_first(): pl.pallas_call(land_kernel, out_shape=[jax.ShapeDtypeStruct((rows, width)...]
    pallas_call x2, Pallas kernels: 87.4 us -> 98.9 us  [forward(): pl.pallas_call(kernel, out_shape=outs, grid_spec=pltpu.PrefetchScalarGrid...]
    dynamic_slice x6 -> x3, local copies, waits for them, and re-layouts: 10.3 us -> 3.16 us  [land(): lax.dynamic_slice_in_dim(value, lax.axis_index(self.stages[0]) * part, part)]
    unnamed x94 -> x112, local copies, waits for them, and re-layouts: 15.3 us -> 11.2 us
  transfers between devices with their start and end apart: 37 -> 37, of which waited for: 14 -> 15; matrix products, arithmetic and copies ran while one was open for 17% -> 11% of each run, Pallas kernels for 30% -> 34%
where the time goes in v3:
time: 550 us; the launch traced here: 540 us
  Pallas kernels  275 us (50%)
  waiting for transfers between devices  103 us (19%)
  starting transfers between devices  55.2 us (10%)
  other arithmetic  45.8 us (8%)
  local copies, waits for them, and re-layouts  41.3 us (8%)
  between operations  18.2 us (3%)
    pallas_call x2, Pallas kernels, forward(): pl.pallas_call(kernel, out_shape=outs, grid_spec=pltpu.PrefetchScalarGrid...  98.9 us
    pallas_call x4, Pallas kernels, feed_back(): pl.pallas_call(kernel, out_shape=outs, grid_spec=pltpu.PrefetchScalarGrid...  85.6 us
    pallas_call x2, Pallas kernels, attention_back(): pl.pallas_call(kernel, out_shape=outs, grid_spec=pltpu.PrefetchScalarGrid...  72.5 us
    all_to_all x7, waiting for transfers between devices, exchange(): return lax.all_to_all(blocks, axes, split_axis=0, concat_axis=0, tiled=True)  65.6 us
    ppermute x28, waiting for transfers between devices, flip(): return lax.ppermute(value, axes, [(i, i ^ amount) for i in range(devices)])  37.7 us
    all_to_all x7, starting transfers between devices, exchange(): return lax.all_to_all(blocks, axes, split_axis=0, concat_axis=0, tiled=True)  29.7 us
    ppermute x28, starting transfers between devices, flip(): return lax.ppermute(value, axes, [(i, i ^ amount) for i in range(devices)])  25.4 us
    pallas_call x3, Pallas kernels, land_first(): pl.pallas_call(land_kernel, out_shape=[jax.ShapeDtypeStruct((rows, width)...  18.1 us
  transfers between devices with their start and end apart: 37, of which 15 were waited for; matrix products, arithmetic and copies ran while one was open for 11% of the time, Pallas kernels for 34%

profile of v3, /device:TPU:0, one launch (start us, length us, event | category | flops | bytes accessed | tf_op | source)
XLA Modules:
  0.0 539.9 jit_solution(8066845914387938759)
XLA Ops:
  26.3 24.7 %shard_map.331 = (bf16[4,512,768]{2,1,0:T(8,128)(2,1)}, bf16[4,512,768]{2,1,0:T(8,128)(2,1)}, bf16[4,512,768]{2,1,0:T(8,128)(2,1)}, bf16[4,512,768]{2,1,0:T(8,12...) custom-call(s32[4]{0:T(128)} %get-tuple-element.238.refs_0_, ...), custom_call_target="tpu_custom_call", output_to_operand_aliasing={{18}: (13, {})} | custom-call | flops 70000001024 | bytes 1000000 | tf_op jit(solution)/shard_map/pallas_call | solution.py:199
  55.0 5.2 collective-permute-done.8
  61.1 74.1 %shard_map.332 = (bf16[4,512,768]{2,1,0:T(8,128)(2,1)}, bf16[4,512,768]{2,1,0:T(8,128)(2,1)}, bf16[4,512,768]{2,1,0:T(8,128)(2,1)}, bf16[4,512,768]{2,1,0:T(8,12...) custom-call(s32[4]{0:T(128)} %get-tuple-element.238.refs_0_, ...), custom_call_target="tpu_custom_call", output_to_operand_aliasing={{0}: (13, {}), {1}: (14, {}), {2}: (15, {}), {3}: (16, {}),... | custom-call | flops 70000001024 | bytes 1000000 | tf_op jit(solution)/shard_map/pallas_call | solution.py:199
  157.9 19.4 %shard_map.333 = (f32[4,512,768]{2,1,0:T(8,128)}, bf16[4,512,768]{2,1,0:T(8,128)(2,1)}, f32[1,768]{1,0:T(1,128)}, f32[8,768]{1,0:T(8,128)}, f32[1536,768]{1,0:T(...) custom-call(s32[4]{0:T(128)} %get-tuple-element.238.refs_0_, ...), custom_call_target="tpu_custom_call", output_to_operand_aliasing={{6}: (10, {}), {7}: (11, {}), {8}: (12, {}), {9}: (13, {})} | custom-call | flops 70000001024 | bytes 1000000 | tf_op jit(solution)/shard_map/pallas_call | solution.py:353
  180.1 19.2 %shard_map.334 = (f32[4,512,768]{2,1,0:T(8,128)}, bf16[4,512,768]{2,1,0:T(8,128)(2,1)}, f32[1,768]{1,0:T(1,128)}, f32[8,768]{1,0:T(8,128)}, f32[1536,768]{1,0:T(...) custom-call(s32[4]{0:T(128)} %get-tuple-element.238.refs_0_, ...), custom_call_target="tpu_custom_call", output_to_operand_aliasing={{4}: (9, {}), {5}: (10, {}), {6}: (11, {})} | custom-call | flops 70000001024 | bytes 1000000 | tf_op jit(solution)/shard_map/pallas_call | solution.py:353
  204.7 19.2 %shard_map.335 = (f32[4,512,768]{2,1,0:T(8,128)}, bf16[4,512,768]{2,1,0:T(8,128)(2,1)}, f32[1,768]{1,0:T(1,128)}, f32[8,768]{1,0:T(8,128)}, f32[1920,768]{1,0:T(...) custom-call(s32[4]{0:T(128)} %get-tuple-element.238.refs_0_, ...), custom_call_target="tpu_custom_call", output_to_operand_aliasing={{6}: (9, {}), {7}: (10, {})} | custom-call | flops 70000001024 | bytes 1000000 | tf_op jit(solution)/shard_map/pallas_call | solution.py:353
  224.8 6.0 %shard_map.336 = (bf16[1536,768]{1,0:T(8,128)(2,1)}, f32[384,768]{1,0:T(8,128)}) custom-call(s32[1]{0:T(128)} %bitcast.16.at, f32[1536,768]{1,0:T(8,128)} %get-tuple-element.164.kept, f32[1536,768]{1,0:T(8,128)} %collective-permute-done.16.came), custom_call_target="tpu_custom_call" | custom-call | flops 1000 | bytes 1000 | tf_op jit(solution)/shard_map/pallas_call | solution.py:552
  234.6 27.8 %shard_map.337 = (f32[4,512,768]{2,1,0:T(8,128)}, bf16[4,512,768]{2,1,0:T(8,128)(2,1)}, f32[1,768]{1,0:T(1,128)}, f32[8,768]{1,0:T(8,128)}, f32[1920,768]{1,0:T(...) custom-call(s32[4]{0:T(128)} %get-tuple-element.238.refs_0_, ...), custom_call_target="tpu_custom_call", output_to_operand_aliasing={{4}: (14, {}), {5}: (15, {}), {6}: (16, {}), {7}: (17, {})} | custom-call | flops 70000001024 | bytes 1000000 | tf_op jit(solution)/shard_map/pallas_call | solution.py:353
  269.0 4.7 all-to-all-start.6
  273.8 36.1 %shard_map.338 = (bf16[4,128,768]{2,1,0:T(8,128)(2,1)}, bf16[4,128,768]{2,1,0:T(8,128)(2,1)}, bf16[4,128,768]{2,1,0:T(8,128)(2,1)}, bf16[4,128,768]{2,1,0:T(8,12...) custom-call(s32[4]{0:T(128)} %get-tuple-element.238.refs_0_, ...), custom_call_target="tpu_custom_call", output_to_operand_aliasing={{6}: (13, {}), {7}: (14, {})} | custom-call | flops 70000001024 | bytes 1000000 | tf_op jit(solution)/shard_map/pallas_call | solution.py:504
  311.7 7.0 %shard_map.339 = (bf16[1920,768]{1,0:T(8,128)(2,1)}, f32[480,768]{1,0:T(8,128)}) custom-call(s32[1]{0:T(128)} %bitcast.16.at, f32[1920,768]{1,0:T(8,128)} %get-tuple-element.184.kept, f32[1920,768]{1,0:T(8,128)} %collective-permute-done.18.came), custom_call_target="tpu_custom_call" | custom-call | flops 1000 | bytes 1000 | tf_op jit(solution)/shard_map/pallas_call | solution.py:552
  318.6 4.1 all-to-all-start.1
  322.7 36.5 %shard_map.340 = (bf16[4,128,768]{2,1,0:T(8,128)(2,1)}, bf16[4,128,768]{2,1,0:T(8,128)(2,1)}, bf16[4,128,768]{2,1,0:T(8,128)(2,1)}, bf16[4,128,768]{2,1,0:T(8,12...) custom-call(s32[4]{0:T(128)} %get-tuple-element.238.refs_0_, ...), custom_call_target="tpu_custom_call", output_to_operand_aliasing={{0}: (14, {}), {1}: (15, {}), {2}: (16, {}), {3}: (17, {}),... | custom-call | flops 70000001024 | bytes 1000000 | tf_op jit(solution)/shard_map/pallas_call | solution.py:504
  373.7 5.1 shard_map.342
  385.5 8.1 %collective-permute-done.25 = f32[120,768]{1,0:T(8,128)S(1)} collective-permute-done((f32[120,768]{1,0:T(8,128)S(1)}, f32[120,768]{1,0:T(8,128)S(1)}, u32[]{:S(2)}, u32[]{:S(2)}) %collective-permute-start.25) | collective-permute-done | bytes 368672 | tf_op jit(solution)/shard_map/ppermute | solution.py:536
  394.3 10.7 %collective-permute-done.26 = f32[120,768]{1,0:T(8,128)} collective-permute-done((f32[120,768]{1,0:T(8,128)S(1)}, f32[120,768]{1,0:T(8,128)}, u32[]{:S(2)}, u32[]{:S(2)}) %collective-permute-start.26) | collective-permute-done | bytes 368672 | tf_op jit(solution)/shard_map/ppermute | solution.py:536
  412.3 6.5 %all-to-all-start.3 = ((bf16[4,32,2304]{2,1,0:T(8,128)(2,1)}), bf16[4,32,2304]{2,1,0:T(8,128)(2,1)S(1)}, u32[]{:S(2)}, u32[]{:S(2)}) async-start(bf16[4,32,2304]{2,1,0:T(8,128)(2,1)} %pad_maximum_fusion.1), calls=%async_computation.3 | async-start | bytes 1179648 | tf_op jit(solution)/shard_map/all_to_all | solution.py:569
  422.0 15.6 %all-to-all-done.3 = bf16[4,32,2304]{2,1,0:T(8,128)(2,1)S(1)} async-done(((bf16[4,32,2304]{2,1,0:T(8,128)(2,1)}), bf16[4,32,2304]{2,1,0:T(8,128)(2,1)S(1)}, u32[]{:S(2)}, u32[]{:S(2)}) %all-to-all-start.3) | async-done | bytes 589856 | tf_op jit(solution)/shard_map/all_to_all | solution.py:569
  443.5 17.4 %all-to-all-done.4 = bf16[4,24,2304]{2,1,0:T(8,128)(2,1)S(1)} async-done(((bf16[4,24,2304]{2,1,0:T(8,128)(2,1)}), bf16[4,24,2304]{2,1,0:T(8,128)(2,1)S(1)}, u32[]{:S(2)}, u32[]{:S(2)}) %all-to-all-start.4) | async-done | bytes 442400 | tf_op jit(solution)/shard_map/all_to_all | solution.py:569
  463.2 3.7 all-to-all-start.5
  467.0 29.9 %all-to-all-done.5 = bf16[4,96,2304]{2,1,0:T(8,128)(2,1)S(1)} async-done(((bf16[4,96,2304]{2,1,0:T(8,128)(2,1)}), bf16[4,96,2304]{2,1,0:T(8,128)(2,1)S(1)}, u32[]{:S(2)}, u32[]{:S(2)}) %all-to-all-start.5) | async-done | bytes 1769504 | tf_op jit(solution)/shard_map/all_to_all | solution.py:569
  510.5 3.8 maximum_select_fusion
  521.0 4.5 maximum_convert_fusion.1
  527.2 4.3 maximum_convert_fusion
  (290 shorter events, 128.2 us)
Async XLA Ops:
  9.4 16.2 %collective-permute-start.3 = (bf16[1,128,768]{2,1,0:T(8,128)(2,1)S(1)}, bf16[1,128,768]{2,1,0:T(8,128)(2,1)S(1)}, u32[]{:S(2)}, u32[]{:S(2)}) collective-permute-start(bf16[1,128,768]{2,1,0:T(8,128)(2,1)S(1)} %get-tuple-element.251), channel_id=1, source_target_pairs={{0,1},{1,0},{2,3},{3,2},{4,5},{5,4},{6,7},{7,6},{8,9},{9,8},{10,11... | collective-permute-start | bytes 589832 | tf_op jit(solution)/shard_map/ppermute | solution.py:536
  9.8 15.8 %collective-permute-start.4 = (bf16[1,128,768]{2,1,0:T(8,128)(2,1)S(1)}, bf16[1,128,768]{2,1,0:T(8,128)(2,1)S(1)}, u32[]{:S(2)}, u32[]{:S(2)}) collective-permute-start(bf16[1,128,768]{2,1,0:T(8,128)(2,1)S(1)} %get-tuple-element.250), channel_id=1, source_target_pairs={{0,2},{1,3},{2,0},{3,1},{4,6},{5,7},{6,4},{7,5},{8,10},{9,11},{10,... | collective-permute-start | bytes 589832 | tf_op jit(solution)/shard_map/ppermute | solution.py:536
  18.7 41.6 %collective-permute-start = (bf16[3,128,768]{2,1,0:T(8,128)(2,1)S(1)}, bf16[3,128,768]{2,1,0:T(8,128)(2,1)S(1)}, u32[]{:S(2)}, u32[]{:S(2)}) collective-permute-start(bf16[3,128,768]{2,1,0:T(8,128)(2,1)S(1)} %get-tuple-element.254), channel_id=1, source_target_pairs={{0,1},{1,0},{2,3},{3,2},{4,5},{5,4},{6,7},{7,6},{8,9},{9,8},{10,11... | collective-permute-start | bytes 1769480 | tf_op jit(solution)/shard_map/ppermute | solution.py:536
  24.1 36.1 %collective-permute-start.1 = (bf16[3,128,768]{2,1,0:T(8,128)(2,1)S(1)}, bf16[3,128,768]{2,1,0:T(8,128)(2,1)}, u32[]{:S(2)}, u32[]{:S(2)}) collective-permute-start(bf16[3,128,768]{2,1,0:T(8,128)(2,1)S(1)} %get-tuple-element.253), channel_id=1, source_target_pairs={{0,2},{1,3},{2,0},{3,1},{4,6},{5,7},{6,4},{7,5},{8,10},{9,11},{10,... | collective-permute-start | bytes 1769480 | tf_op jit(solution)/shard_map/ppermute | solution.py:536
  25.6 34.6 %collective-permute-start.2 = (bf16[3,128,768]{2,1,0:T(8,128)(2,1)S(1)}, bf16[3,128,768]{2,1,0:T(8,128)(2,1)}, u32[]{:S(2)}, u32[]{:S(2)}) collective-permute-start(bf16[3,128,768]{2,1,0:T(8,128)(2,1)S(1)} %get-tuple-element.252), channel_id=1, source_target_pairs={{0,3},{1,2},{2,1},{3,0},{4,7},{5,6},{6,5},{7,4},{8,11},{9,10},{10,... | collective-permute-start | bytes 1769480 | tf_op jit(solution)/shard_map/ppermute | solution.py:536
  177.2 26.5 %collective-permute-start.14 = (bf16[4,128,768]{2,1,0:T(8,128)(2,1)}, bf16[4,128,768]{2,1,0:T(8,128)(2,1)S(1)}, u32[]{:S(2)}, u32[]{:S(2)}) collective-permute-start(bf16[4,128,768]{2,1,0:T(8,128)(2,1)} %get-tuple-element.154), channel_id=1, source_target_pairs={{0,1},{1,0},{2,3},{3,2},{4,5},{5,4},{6,7},{7,6},{8,9},{9,8},{10,11... | collective-permute-start | bytes 2359304 | tf_op jit(solution)/shard_map/ppermute | solution.py:536
  199.3 25.5 %collective-permute-start.16 = (f32[1536,768]{1,0:T(8,128)}, f32[1536,768]{1,0:T(8,128)}, u32[]{:S(2)}, u32[]{:S(2)}) collective-permute-start(f32[1536,768]{1,0:T(8,128)} %get-tuple-element.165), channel_id=1, source_target_pairs={{0,1},{1,0},{2,3},{3,2},{4,5},{5,4},{6,7},{7,6},{8,9},{9,8},{10,11... | collective-permute-start | bytes 14155784 | tf_op jit(solution)/shard_map/ppermute | solution.py:536
  199.4 24.5 %collective-permute-start.15 = (bf16[4,128,768]{2,1,0:T(8,128)(2,1)}, bf16[4,128,768]{2,1,0:T(8,128)(2,1)S(1)}, u32[]{:S(2)}, u32[]{:S(2)}) collective-permute-start(bf16[4,128,768]{2,1,0:T(8,128)(2,1)} %get-tuple-element.163), channel_id=1, source_target_pairs={{0,2},{1,3},{2,0},{3,1},{4,6},{5,7},{6,4},{7,5},{8,10},{9,11},{10,... | collective-permute-start | bytes 2359304 | tf_op jit(solution)/shard_map/ppermute | solution.py:536
  203.3 297.2 %collective-permute-start.17 = (bf16[4,128,768]{2,1,0:T(8,128)(2,1)}, bf16[4,128,768]{2,1,0:T(8,128)(2,1)}, u32[]{:S(2)}, u32[]{:S(2)}) collective-permute-start(bf16[4,128,768]{2,1,0:T(8,128)(2,1)} %get-tuple-element.168), channel_id=1, source_target_pairs={{0,3},{1,2},{2,1},{3,0},{4,7},{5,6},{6,5},{7,4},{8,11},{9,10},{10,... | collective-permute-start | bytes 2359304 | tf_op jit(solution)/shard_map/ppermute | solution.py:536
  230.9 34.6 %all-to-all-start = ((bf16[4,384,768]{2,1,0:T(8,128)(2,1)}), bf16[4,384,768]{2,1,0:T(8,128)(2,1)S(1)}, u32[]{:S(2)}, u32[]{:S(2)}) async-start(bf16[4,384,768]{2,1,0:T(8,128)(2,1)} %bitcast.94), calls=%async_computation | async-start | bytes 4718592 | tf_op jit(solution)/shard_map/all_to_all | solution.py:569
  262.4 49.3 %collective-permute-start.18 = (f32[1920,768]{1,0:T(8,128)}, f32[1920,768]{1,0:T(8,128)}, u32[]{:S(2)}, u32[]{:S(2)}) collective-permute-start(f32[1920,768]{1,0:T(8,128)} %get-tuple-element.185), channel_id=1, source_target_pairs={{0,1},{1,0},{2,3},{3,2},{4,5},{5,4},{6,7},{7,6},{8,9},{9,8},{10,11... | collective-permute-start | bytes 17694728 | tf_op jit(solution)/shard_map/ppermute | solution.py:536
  269.0 40.8 %all-to-all-start.6 = ((f32[4,96,768]{2,1,0:T(8,128)}), f32[4,96,768]{2,1,0:T(8,128)S(1)}, u32[]{:S(2)}, u32[]{:S(2)}) async-start(f32[4,96,768]{2,1,0:T(8,128)} %bitcast.37), calls=%async_computation.6 | async-start | bytes 2359296 | tf_op jit(solution)/shard_map/all_to_all | solution.py:569
  273.8 232.0 %all-gather.5.cloned.1.call-start = ((), (), s32[]{:S(2)}) async-start(), calls=%async_computation.8 | async-start | bytes 4866048 | tf_op jit(solution)/shard_map/all_gather | solution.py:896
  318.6 48.1 %all-to-all-start.1 = ((bf16[4,480,768]{2,1,0:T(8,128)(2,1)}), bf16[4,480,768]{2,1,0:T(8,128)(2,1)S(1)}, u32[]{:S(2)}, u32[]{:S(2)}) async-start(bf16[4,480,768]{2,1,0:T(8,128)(2,1)} %bitcast.93), calls=%async_computation.1 | async-start | bytes 5898240 | tf_op jit(solution)/shard_map/all_to_all | solution.py:569
  360.7 58.8 %collective-permute-start.21 = (bf16[4,128,768]{2,1,0:T(8,128)(2,1)}, bf16[4,128,768]{2,1,0:T(8,128)(2,1)}, u32[]{:S(2)}, u32[]{:S(2)}) collective-permute-start(bf16[4,128,768]{2,1,0:T(8,128)(2,1)} %get-tuple-element.206), channel_id=1, source_target_pairs={{0,2},{1,3},{2,0},{3,1},{4,6},{5,7},{6,4},{7,5},{8,10},{9,11},{10,... | collective-permute-start | bytes 2359304 | tf_op jit(solution)/shard_map/ppermute | solution.py:536
  369.2 24.4 %collective-permute-start.25 = (f32[120,768]{1,0:T(8,128)S(1)}, f32[120,768]{1,0:T(8,128)S(1)}, u32[]{:S(2)}, u32[]{:S(2)}) collective-permute-start(f32[120,768]{1,0:T(8,128)S(1)} %get-tuple-element.256), channel_id=1, source_target_pairs={{0,8},{8,0},{16,24},{24,16},{1,9},{9,1},{17,25},{25,17},{2,10},{10... | collective-permute-start | bytes 1105928 | tf_op jit(solution)/shard_map/ppermute | solution.py:536
  371.3 33.7 %collective-permute-start.26 = (f32[120,768]{1,0:T(8,128)S(1)}, f32[120,768]{1,0:T(8,128)}, u32[]{:S(2)}, u32[]{:S(2)}) collective-permute-start(f32[120,768]{1,0:T(8,128)S(1)} %get-tuple-element.258), channel_id=1, source_target_pairs={{0,16},{8,24},{16,0},{24,8},{1,17},{9,25},{17,1},{25,9},{2,18},{10... | collective-permute-start | bytes 1105928 | tf_op jit(solution)/shard_map/ppermute | solution.py:536
  373.6 31.4 %collective-permute-start.27 = (f32[120,768]{1,0:T(8,128)S(1)}, f32[120,768]{1,0:T(8,128)}, u32[]{:S(2)}, u32[]{:S(2)}) collective-permute-start(f32[120,768]{1,0:T(8,128)S(1)} %get-tuple-element.257), channel_id=1, source_target_pairs={{0,24},{8,16},{16,8},{24,0},{1,25},{9,17},{17,9},{25,1},{2,26},{10... | collective-permute-start | bytes 1105928 | tf_op jit(solution)/shard_map/ppermute | solution.py:536
  381.8 28.0 %all-to-all-start.2 = ((bf16[4,104,2304]{2,1,0:T(8,128)(2,1)}), bf16[4,104,2304]{2,1,0:T(8,128)(2,1)S(1)}, u32[]{:S(2)}, u32[]{:S(2)}) async-start(bf16[4,104,2304]{2,1,0:T(8,128)(2,1)} %pad_maximum_fusion), calls=%async_computation.2 | async-start | bytes 3833856 | tf_op jit(solution)/shard_map/all_to_all | solution.py:569
  385.4 132.0 %all-gather.3.cloned.1.call-start = ((), (), s32[]{:S(2)}) async-start(), calls=%async_computation.7 | async-start | bytes 6082560 | tf_op jit(solution)/shard_map/all_gather | solution.py:896
  394.3 47.9 %collective-permute-start.22 = (bf16[4,128,768]{2,1,0:T(8,128)(2,1)}, bf16[4,128,768]{2,1,0:T(8,128)(2,1)S(1)}, u32[]{:S(2)}, u32[]{:S(2)}) collective-permute-start(bf16[4,128,768]{2,1,0:T(8,128)(2,1)} %get-tuple-element.209), channel_id=1, source_target_pairs={{0,3},{1,2},{2,1},{3,0},{4,7},{5,6},{6,5},{7,4},{8,11},{9,10},{10,... | collective-permute-start | bytes 2359304 | tf_op jit(solution)/shard_map/ppermute | solution.py:536
  412.3 25.4 %all-to-all-start.3 = ((bf16[4,32,2304]{2,1,0:T(8,128)(2,1)}), bf16[4,32,2304]{2,1,0:T(8,128)(2,1)S(1)}, u32[]{:S(2)}, u32[]{:S(2)}) async-start(bf16[4,32,2304]{2,1,0:T(8,128)(2,1)} %pad_maximum_fusion.1), calls=%async_computation.3 | async-start | bytes 1179648 | tf_op jit(solution)/shard_map/all_to_all | solution.py:569
  438.7 22.2 %all-to-all-start.4 = ((bf16[4,24,2304]{2,1,0:T(8,128)(2,1)}), bf16[4,24,2304]{2,1,0:T(8,128)(2,1)S(1)}, u32[]{:S(2)}, u32[]{:S(2)}) async-start(bf16[4,24,2304]{2,1,0:T(8,128)(2,1)} %broadcast_in_dim.287), calls=%async_computation.4 | async-start | bytes 884736 | tf_op jit(solution)/shard_map/all_to_all | solution.py:569
  463.2 33.6 %all-to-all-start.5 = ((bf16[4,96,2304]{2,1,0:T(8,128)(2,1)}), bf16[4,96,2304]{2,1,0:T(8,128)(2,1)S(1)}, u32[]{:S(2)}, u32[]{:S(2)}) async-start(bf16[4,96,2304]{2,1,0:T(8,128)(2,1)} %broadcast_in_dim.292), calls=%async_computation.5 | async-start | bytes 3538944 | tf_op jit(solution)/shard_map/all_to_all | solution.py:569
  (59 other events, 747.5 us)
Sparse Core Ops, SparseCore 0:
  311.8 94.3 all-gather.4
  409.0 97.0 all-gather.2
